TPU v7x, 512 devices: a whole 4x4x16 slice. The times are simulated.
512 devices in a mesh: seq: 64 (over x, z_hi, y, core), head: 8 (over z_lo).
Axes of the slice: x: 4, y: 4, z: 16 (z_hi: 2, z_lo: 8; z = z_hi * 8 + z_lo), core: 2. Of those that a mesh axis runs over, the one named last changes fastest.
Arguments:
- queries: bfloat16 [32768, 3072], P('seq', 'head'), may hold values from -120 to 120
- encodings: bfloat16 [64, 256, 4096], P('seq', None, 'head'), may hold values from -6 to 6
- key_weight: bfloat16 [4096, 3072], P('seq', 'head'), may hold values from -0.09375 to 0.09375
- value_weight: bfloat16 [4096, 3072], P('seq', 'head'), may hold values from -0.09375 to 0.09375
- text_length: int32 [64], P('seq'), may hold values from 1 to 256
- image_offset: int32 [64], P('seq'), may hold values from 0 to 511, as said below
- cotangent: bfloat16 [32768, 3072], P('seq', 'head'), may hold values from -6 to 6
Outputs:
- attended: bfloat16 [32768, 3072], P('seq', 'head')
- query_grad: bfloat16 [32768, 3072], P('seq', 'head')
- encoding_grad: bfloat16 [64, 256, 4096], P('seq', None, 'head')
Inputs may be any that keep to these rules, and one draw needn't show every extreme that they name: The image tokens of prompt p begin at p * 512 + image_offset[p] and run up to where those of prompt p + 1 begin, the last prompt's to the end; image_offset[0] is 0.
All inputs are finite; a program needn't handle non-finite values.
Results may differ from a plain program's by a relative error of at most 0.018.
The roundings to bfloat16 on the way count: a program that leaves them out, or rounds other values in their place, can miss the bound.
Values may be sent and summed in bfloat16 or wider, within the bound.
A program may use at most 64 MiB of HBM per device.

v0:
```python
import math

import jax
import jax.numpy as jnp
from jax import lax
from jax.sharding import PartitionSpec as P

HD = 128


def passed_along(value, axis, steps):
    count = lax.axis_size(axis)
    leading, last = (max(0, -steps), min(count, count - steps))
    return lax.ppermute(value, axis, [(source, source + steps) for source in range(leading, last)])


def attend_local(queries, cotangent, keys, values, allowed, heads_here):
    scale = 1.0 / math.sqrt(HD)
    tokens_here = queries.shape[0]
    q = queries.reshape(tokens_here, heads_here, HD)
    g = cotangent.reshape(tokens_here, heads_here, HD)
    k = keys.reshape(keys.shape[0], heads_here, HD)
    v = values.reshape(values.shape[0], heads_here, HD)
    scores = jnp.einsum("thd,khd->htk", q, k, preferred_element_type=jnp.float32) * scale
    masked = jnp.where(allowed[None], scores, jnp.float32(-1e30))
    top = jnp.max(masked, axis=-1, keepdims=True)
    expo = jnp.exp(masked - top)
    probs = expo / jnp.sum(expo, axis=-1, keepdims=True)
    probs_b = probs.astype(jnp.bfloat16)
    out = jnp.einsum("htk,khd->thd", probs_b, v, preferred_element_type=jnp.float32).astype(
        jnp.bfloat16
    )
    dprobs = jnp.einsum("thd,khd->htk", g, v, preferred_element_type=jnp.float32)
    delta = jnp.sum(probs * dprobs, axis=-1, keepdims=True)
    dscores = (probs * (dprobs - delta) * scale).astype(jnp.bfloat16)
    dq = jnp.einsum("htk,khd->thd", dscores, k, preferred_element_type=jnp.float32).astype(
        jnp.bfloat16
    )
    dk = jnp.einsum("htk,thd->khd", dscores, q, preferred_element_type=jnp.float32)
    dv = jnp.einsum("htk,thd->khd", probs_b, g, preferred_element_type=jnp.float32)
    width = heads_here * HD
    return (
        out.reshape(tokens_here, width),
        dq.reshape(tokens_here, width),
        dk.reshape(-1, width),
        dv.reshape(-1, width),
    )


def shards(queries, encodings, key_weight, value_weight, text_length, image_offset, cotangent):
    width = queries.shape[1]
    heads_here = width // HD
    lmax = encodings.shape[1]
    key_full, value_full = (
        lax.all_gather(key_weight, "seq", axis=0, tiled=True),
        lax.all_gather(value_weight, "seq", axis=0, tiled=True),
    )
    own_valid = (jnp.arange(lmax, dtype=jnp.int32) < text_length[0]).astype(jnp.bfloat16)
    prev_enc, prev_valid = passed_along((encodings, own_valid), "seq", 1)
    both_rows = jnp.concatenate([prev_enc[0], encodings[0]], 0)
    full_rows = lax.all_gather(both_rows, "head", axis=1, tiled=True)
    keys = jnp.dot(full_rows, key_full, preferred_element_type=jnp.float32)
    values = jnp.dot(full_rows, value_full, preferred_element_type=jnp.float32)
    keys, values = (keys.astype(jnp.bfloat16), values.astype(jnp.bfloat16))
    tokens_here = queries.shape[0]
    own_row = (jnp.arange(tokens_here, dtype=jnp.int32) >= image_offset[0])[:, None]
    prev_ok = (prev_valid > 0.5)[None, :]
    own_ok = (own_valid > 0.5)[None, :]
    allowed = jnp.concatenate(
        [jnp.logical_and(jnp.logical_not(own_row), prev_ok), jnp.logical_and(own_row, own_ok)], 1
    )
    attended, query_grad, dk, dv = attend_local(
        queries, cotangent, keys, values, allowed, heads_here
    )
    back_keys, back_values = passed_along((dk[:lmax], dv[:lmax]), "seq", -1)
    key_grad = (dk[lmax:] + back_keys).astype(jnp.bfloat16)
    value_grad = (dv[lmax:] + back_values).astype(jnp.bfloat16)
    key_rows, value_rows = (key_full, value_full)
    partial_grad = lax.dot_general(
        key_grad, key_rows, (((1,), (1,)), ((), ())), preferred_element_type=jnp.float32
    )
    partial_grad = partial_grad + lax.dot_general(
        value_grad, value_rows, (((1,), (1,)), ((), ())), preferred_element_type=jnp.float32
    )
    summed = lax.psum_scatter(
        partial_grad.astype(jnp.bfloat16), "head", scatter_dimension=1, tiled=True
    )
    encoding_grad = summed[None]
    return (attended, query_grad, encoding_grad)


def solution(mesh):
    return jax.shard_map(
        shards,
        mesh=mesh,
        in_specs=(
            P("seq", "head"),
            P("seq", None, "head"),
            P("seq", "head"),
            P("seq", "head"),
            P("seq"),
            P("seq"),
            P("seq", "head"),
        ),
        out_specs=(P("seq", "head"), P("seq", "head"), P("seq", None, "head")),
        check_vma=False,
    )
```

profile of v0, /device:TPU:24, one launch (start us, length us, event | category | flops | bytes accessed | tf_op | source)
XLA Modules:
  0.0 483.0 jit_solution(2799952289683187256)
XLA Ops:
  7.2 0.7 all-gather.8.cloned.1.call-update
  7.9 1.9 collective-permute-start
  9.9 6.0 %collective-permute-done = bf16[1,256,512]{2,1,0:T(8,128)(2,1)S(1)} collective-permute-done((bf16[1,256,512]{2,1,0:T(8,128)(2,1)}, bf16[1,256,512]{2,1,0:T(8,128)(2,1)S(1)}, u32[]{:S(2)}, u32[]{:S(2)}) %collective-permute-start) | collective-permute-done | bytes 262176 | tf_op jit(solution)/shard_map/ppermute | solution.py:14
  15.8 1.8 pad_maximum_fusion
  17.7 0.7 all-gather.6.cloned.1.call-update
  19.1 20.5 %collective-permute-start.1 = (bf16[256]{0:T(256)(128)(2,1)S(1)}, bf16[256]{0:T(256)(128)(2,1)S(1)}, u32[]{:S(2)}, u32[]{:S(2)}) collective-permute-start(bf16[256]{0:T(256)(128)(2,1)S(1)} %compare_convert_fusion), channel_id=1, source_target_pairs={{0,8},{8,16},{16,24},{24,32},{32,40},{40,48},{48,56},{56,64},{64,7... | collective-permute-start | bytes 1544 | tf_op jit(solution)/shard_map/ppermute | solution.py:14
  40.3 0.1 broadcast_and_fusion
  40.5 1.2 copy.23
  41.6 1.3 copy.28
  43.1 93.9 %all-gather.8.cloned.1.call-done = bf16[4096,384]{1,0:T(8,128)(2,1)} async-done(((bf16[64,384]{1,0:T(8,128)(2,1)}), bf16[4096,384]{1,0:T(8,128)(2,1)}) %all-gather.8.cloned.1.call-update) | async-done | bytes 3145744 | tf_op jit(solution)/shard_map/all_gather | solution.py:55
  137.1 97.5 %all-gather.4.cloned.1.call-done = bf16[512,4096]{1,0:T(8,128)(2,1)} async-done(((bf16[512,512]{1,0:T(8,128)(2,1)}), bf16[512,4096]{1,0:T(8,128)(2,1)}) %all-gather.4.cloned.1.call-update) | async-done | bytes 4194320 | tf_op jit(solution)/shard_map/all_gather | solution.py:61
  234.6 5.0 %convolution_convert_fusion.1 = bf16[512,384]{0,1:T(8,128)(2,1)S(1)} fusion(bf16[512,4096]{1,0:T(8,128)(2,1)} %all-gather.4.cloned.1.call-done, bf16[4096,384]{1,0:T(8,128)(2,1)} %all-gather.8.cloned.1.call-done), kind=kOutput, calls=%fused_computation.23 | convolution fusion | flops 1610809344 | bytes 7733248 | tf_op jit(solution)/shard_map/dot_general | solution.py:62
  239.6 3.1 fusion.30
  242.7 2.5 convolution_bitcast_fusion
  245.3 0.8 fusion.29
  246.1 1.9 collective-permute-start.3
  248.0 115.6 %all-gather.6.cloned.1.call-done = bf16[4096,384]{1,0:T(8,128)(2,1)} async-done(((bf16[64,384]{1,0:T(8,128)(2,1)}), bf16[4096,384]{1,0:T(8,128)(2,1)}) %all-gather.6.cloned.1.call-update) | async-done | bytes 3145744 | tf_op jit(solution)/shard_map/all_gather | solution.py:56
  363.6 5.0 %convolution_convert_fusion.2 = bf16[512,384]{0,1:T(8,128)(2,1)S(1)} fusion(bf16[512,4096]{1,0:T(8,128)(2,1)} %all-gather.4.cloned.1.call-done, bf16[4096,384]{1,0:T(8,128)(2,1)} %all-gather.6.cloned.1.call-done), kind=kOutput, calls=%fused_computation.24 | convolution fusion | flops 1610809344 | bytes 7733248 | tf_op jit(solution)/shard_map/dot_general | solution.py:63
  368.6 0.7 copy-done.3
  369.4 2.2 fusion.31
  371.6 7.2 %fusion.13 = f32[512,3,128]{0,2,1:T(8,128)} fusion(bf16[512,3,128]{0,2,1:T(8,128)(2,1)} %bitcast.92, f32[3,512,512]{2,1,0:T(8,128)} %fusion.31, f32[3,512,512]{1,2,0:T(8,128)} %get-tuple-element.14, f32[3,512]{1,0:T(4,128)S(1)} %get-tuple-element.13), kind=kOutput, calls=%fused_computation.19 | convolution fusion | flops 206833664 | bytes 7477248 | tf_op jit(solution)/shard_map/htk,thd->khd/dot_general | solution.py:39
  378.8 1.2 fusion.28
  380.0 3.1 collective-permute-start.2
  383.1 1.0 fusion.17
  384.1 1.3 fusion.32
  385.4 2.7 collective-permute-done.2
  388.2 2.7 fusion.2
  390.9 2.3 convolution_convert_fusion
  393.3 0.9 copy.34
  394.2 6.4 %fusion.14 = bf16[3,128,512]{2,1,0:T(8,128)(2,1)S(1)} fusion(bf16[512,3,128]{0,2,1:T(8,128)(2,1)S(1)} %bitcast.102, f32[3,512,512]{2,1,0:T(8,128)} %fusion.31, f32[3,512,512]{1,2,0:T(8,128)} %get-tuple-element.14, f32[3,512]{1,0:T(4,128)S(1)} %get-tuple-element.13), kind=kOutput, calls=%fused_computation.21 | convolution fusion | flops 207030272 | bytes 7084032 | tf_op jit(solution)/shard_map/htk,khd->thd/dot_general | solution.py:36
  400.6 0.9 copy.35
  401.5 74.9 %reduce-scatter.2.cloned.1.call-done = bf16[256,512]{1,0:T(8,128)(2,1)} async-done(((bf16[256,4096]{1,0:T(8,128)(2,1)}), bf16[256,512]{1,0:T(8,128)(2,1)}) %reduce-scatter.2.cloned.1.call-update) | async-done | bytes 262160 | tf_op jit(solution)/shard_map/reduce_scatter | solution.py:85
  (28 shorter events, 0.4 us)
Async XLA Ops:
  7.2 129.9 %all-gather.8.cloned.1.call-start = ((), (), s32[]{:S(2)}) async-start(), calls=%async_computation.3 | async-start | bytes 3194880 | tf_op jit(solution)/shard_map/all_gather | solution.py:55
  7.9 226.7 %all-gather.4.cloned.1.call-start = ((), (), s32[]{:S(2)}) async-start(), calls=%async_computation.1 | async-start | bytes 4718592 | tf_op jit(solution)/shard_map/all_gather | solution.py:61
  7.9 7.9 %collective-permute-start = (bf16[1,256,512]{2,1,0:T(8,128)(2,1)}, bf16[1,256,512]{2,1,0:T(8,128)(2,1)S(1)}, u32[]{:S(2)}, u32[]{:S(2)}) collective-permute-start(bf16[1,256,512]{2,1,0:T(8,128)(2,1)} %param.8), channel_id=1, source_target_pairs={{0,8},{8,16},{16,24},{24,32},{32,40},{40,48},{48,56},{56,64},{64,7... | collective-permute-start | bytes 786440 | tf_op jit(solution)/shard_map/ppermute | solution.py:14
  17.7 345.9 %all-gather.6.cloned.1.call-start = ((), (), s32[]{:S(2)}) async-start(), calls=%async_computation.2 | async-start | bytes 3194880 | tf_op jit(solution)/shard_map/all_gather | solution.py:56
  18.4 458.0 %reduce-scatter.2.cloned.1.call-start = ((), (), s32[]{:S(2)}) async-start(), calls=%async_computation.4 | async-start | bytes 2359296 | tf_op jit(solution)/shard_map/reduce_scatter | solution.py:85
  19.1 23.9 %collective-permute-start.1 = (bf16[256]{0:T(256)(128)(2,1)S(1)}, bf16[256]{0:T(256)(128)(2,1)S(1)}, u32[]{:S(2)}, u32[]{:S(2)}) collective-permute-start(bf16[256]{0:T(256)(128)(2,1)S(1)} %compare_convert_fusion), channel_id=1, source_target_pairs={{0,8},{8,16},{16,24},{24,32},{32,40},{40,48},{48,56},{56,64},{64,7... | collective-permute-start | bytes 1544 | tf_op jit(solution)/shard_map/ppermute | solution.py:14
  41.6 201.1 %copy-start.2 = (bf16[512,384]{0,1:T(8,128)(2,1)}, bf16[512,384]{0,1:T(8,128)(2,1)S(1)}, u32[]{:S(2)}) copy-start(bf16[512,384]{0,1:T(8,128)(2,1)S(1)} %copy.23) | copy-start | bytes 1179652
  239.6 5.7 %copy-start.5 = (bf16[512,384]{0,1:T(8,128)(2,1)}, bf16[512,384]{0,1:T(8,128)(2,1)S(1)}, u32[]{:S(2)}) copy-start(bf16[512,384]{0,1:T(8,128)(2,1)S(1)} %convolution_convert_fusion.1) | copy-start | bytes 1179652
  246.1 136.9 %collective-permute-start.3 = (f32[256,384]{0,1:T(8,128)}, f32[256,384]{0,1:T(8,128)}, u32[]{:S(2)}, u32[]{:S(2)}) collective-permute-start(f32[256,384]{0,1:T(8,128)} %bitcast.19), channel_id=1, source_target_pairs={{8,0},{16,8},{24,16},{32,24},{40,32},{48,40},{56,48},{64,56},{72,6... | collective-permute-start | bytes 1179656 | tf_op jit(solution)/shard_map/ppermute | solution.py:14
  368.6 0.7 copy-start.3
  371.6 12.5 %copy-start = (bf16[4096,384]{1,0:T(8,128)(2,1)S(1)}, bf16[4096,384]{1,0:T(8,128)(2,1)}, u32[]{:S(2)}) copy-start(bf16[4096,384]{1,0:T(8,128)(2,1)} %all-gather.6.cloned.1.call-done) | copy-start | bytes 9437188
  380.0 8.2 %collective-permute-start.2 = (f32[256,384]{0,1:T(8,128)S(1)}, f32[256,384]{0,1:T(8,128)S(1)}, u32[]{:S(2)}, u32[]{:S(2)}) collective-permute-start(f32[256,384]{0,1:T(8,128)S(1)} %bitcast.95), channel_id=1, source_target_pairs={{8,0},{16,8},{24,16},{32,24},{40,32},{48,40},{56,48},{64,56},{72,6... | collective-permute-start | bytes 1179656 | tf_op jit(solution)/shard_map/ppermute | solution.py:14
  384.1 4.1 copy-start.1
  388.2 2.7 copy-start.4
  390.9 3.3 copy-start.6
Sparse Core Ops, SparseCore 0:
  12.5 124.5 all-gather.7
  139.1 95.4 all-gather.3
  239.1 124.4 all-gather.5
  391.0 85.3 reduce-scatter.1
where the time goes:
time: 484 us; the launch traced here: 483 us
  waiting for transfers between devices  392 us (81%)
  matrix products  37.7 us (8%)
  starting transfers between devices  27.6 us (6%)
  between operations  15.3 us (3%)
  local copies, waits for them, and re-layouts  7.08 us (1%)
    all_gather x1, waiting for transfers between devices, shards(): lax.all_gather(value_weight, 'seq', axis=0, tiled=True)  116 us
    all_gather x1, waiting for transfers between devices, shards(): full_rows = lax.all_gather(both_rows, 'head', axis=1, tiled=True)  97.5 us
    all_gather x1, waiting for transfers between devices, shards(): lax.all_gather(key_weight, 'seq', axis=0, tiled=True)  93.9 us
    reduce_scatter x1, waiting for transfers between devices, shards(): lax.psum_scatter(partial_grad.astype(jnp.bfloat16), 'head', scatter_dimen...  74.9 us
    ppermute x4, starting transfers between devices, passed_along(): lax.ppermute(value, axis, [(source, source + steps) for source in range(l...  27.5 us
  transfers between devices with their start and end apart: 8, of which 6 were waited for; matrix products, arithmetic and copies ran while one was open for 9% of the time, Pallas kernels for 0%

commit v1 on v0

v1 whole, which is shorter than its diff:
```python
import functools
import math

import jax
import jax.numpy as jnp
from jax import lax
from jax.experimental import pallas as pl
from jax.experimental.pallas import tpu as pltpu
from jax.sharding import PartitionSpec as P

HD = 128
GRID = (4, 2, 4, 2)
CHUNKS = 2
BF = jnp.bfloat16
F32 = jnp.float32
MESH = pl.DeviceIdType.MESH


def dot(a, b, da, db):
    return lax.dot_general(a, b, (((da,), (db,)), ((), ())), preferred_element_type=F32)


def kernel(
    dims, len_ref, off_ref, q_ref, g_ref, enc_ref, wk_ref, wv_ref,
    out_ref, dq_ref, de_ref,
    w, wmid, enc, kv, valid, ra, rm, rc, ba, bm, bc, dk32, dprev, dback, dkv, rr, rl, proj,
    ws1, wr1, ws2, wr2, wsx, wrx, wsb, wrb,
    esr, err, esl, erl, vs, vr,
    ks, kr, ps, pr, cs, cr, fs, fr,
    bks, bkr, bps, bpr, bcs, bcr, bfs, bfr,
    rsr, rrr, rsl, rrl,
):
    nx, nh, ny, nc, nz = dims
    width = wk_ref.shape[1]
    heads = width // HD
    lmax = enc_ref.shape[1]
    tokens = q_ref.shape[0]
    piece = lmax // ny
    rows = lmax // CHUNKS
    s = lax.axis_index("seq")
    h = lax.axis_index("head")
    c = s % nc
    y = (s // nc) % ny
    zh = (s // (nc * ny)) % nh
    x = s // (nc * ny * nh)
    last = nx * nh * ny * nc - 1

    def at(x_, zh_, y_, c_):
        return ((x_ * nh + zh_) * ny + y_) * nc + c_

    def along(steps):
        z = (zh * nz + h + steps + nh * nz) % (nh * nz)
        return (at(x, z // nz, y, c), z % nz), z // nz

    sib = (at(x, zh, y, 1 - c), h)
    up, zh_up = along(nz // 2)
    down, zh_down = along(-(nz // 2))
    xs = [(at((x + d) % nx, zh, y, c), h) for d in range(1, nx)]
    ys = [(at(x, zh, (y + d) % ny, c), h) for d in range(1, ny)]
    right = (s, h + 1)
    left = (s, h - 1)
    KC, VC = slice(0, width), slice(width, 2 * width)

    has_next = s < last
    has_prev = s > 0
    far_next = jnp.logical_and(c == nc - 1, y == ny - 1)
    far_prev = jnp.logical_and(c == 0, y == 0)
    relay = c == nc - 1
    serves = jnp.logical_and(relay, jnp.logical_or(zh == 1, x < nx - 1))
    served_x = jnp.where(zh == 1, x, x + 1)
    goes = jnp.logical_and(relay, jnp.logical_not(jnp.logical_and(zh == 1, x == nx - 1)))
    source_x = jnp.where(zh == 1, x, x - 1)

    def when(*conds):
        return pl.when(functools.reduce(jnp.logical_and, conds))

    def copy(src, dst, ss, rs, dev):
        return pltpu.make_async_remote_copy(
            src_ref=src, dst_ref=dst, send_sem=ss, recv_sem=rs, device_id=dev, device_id_type=MESH
        )

    barrier = pltpu.get_barrier_semaphore()

    def hello(dev):
        pl.semaphore_signal(barrier, inc=1, device_id=dev, device_id_type=MESH)

    for dev in [sib, up, down] + xs + ys:
        hello(dev)

    @when(h < nz - 1)
    def _():
        hello(right)

    @when(h > 0)
    def _():
        hello(left)

    @when(has_next)
    def _():
        hello((s + 1, h))

    @when(has_prev)
    def _():
        hello((s - 1, h))

    @when(serves)
    def _():
        hello((at(served_x, zh, 0, 0), h))

    @when(far_prev, has_prev)
    def _():
        for i in range(ny):
            hello((at(source_x, zh, i, nc - 1), h))

    w[x, zh, y, c, :, KC] = wk_ref[...]
    w[x, zh, y, c, :, VC] = wv_ref[...]
    enc[h] = enc_ref[0]
    columns = lax.broadcasted_iota(jnp.int32, (8, lmax), 1)
    valid[1] = (columns < len_ref[0]).astype(F32)

    @when(s == 0)
    def _():
        valid[0] = jnp.ones((8, lmax), F32)
        kv[0] = jnp.zeros((lmax, 2 * width), BF)

    @when(s == last)
    def _():
        dback[...] = jnp.zeros_like(dback)

    @when(h == 0)
    def _():
        rr[...] = jnp.zeros_like(rr)

    @when(h == nz - 1)
    def _():
        rl[...] = jnp.zeros_like(rl)

    count = 3 + (nx - 1) + (ny - 1)
    count = count + (h < nz - 1).astype(jnp.int32) + (h > 0).astype(jnp.int32)
    count = count + has_next.astype(jnp.int32) + has_prev.astype(jnp.int32)
    count = count + serves.astype(jnp.int32)
    count = count + ny * jnp.logical_and(far_prev, has_prev).astype(jnp.int32)
    pl.semaphore_wait(barrier, count)

    def cross_up(i, leg):
        if i == 0:
            if leg == 0:
                return copy(w.at[x, zh, y, c, :, KC], wmid.at[:, KC], wsx.at[0], wrx.at[0], up)
            return copy(wmid.at[:, KC], w.at[x, zh_down, y, c, :, KC], wsx.at[1], wrx.at[1], up)
        if leg == 0:
            return copy(w.at[x, zh, y, c, :, VC], wmid.at[:, VC], wsx.at[2], wrx.at[2], down)
        return copy(wmid.at[:, VC], w.at[x, zh_up, y, c, :, VC], wsx.at[3], wrx.at[3], down)

    def first(which, z_, d):
        if which == 0:
            ref = w.at[x, z_, y, c, :, KC]
            return copy(ref, ref, ws1.at[0, d - 1, z_], wr1.at[0, d - 1, z_], xs[d - 1])
        ref = w.at[x, z_, y, c, :, VC]
        return copy(ref, ref, ws1.at[1, d - 1, z_], wr1.at[1, d - 1, z_], ys[d - 1])

    def second(which, z_, d):
        if which == 0:
            ref = w.at[:, z_, y, c, :, KC]
            return copy(ref, ref, ws2.at[0, d - 1, z_], wr2.at[0, d - 1, z_], ys[d - 1])
        ref = w.at[x, z_, :, c, :, VC]
        return copy(ref, ref, ws2.at[1, d - 1, z_], wr2.at[1, d - 1, z_], xs[d - 1])

    def share(z_):
        ref = w.at[:, z_, :, c]
        return copy(ref, ref, wsb.at[z_], wrb.at[z_], sib)

    def each(make, z_, act):
        for d in range(1, max(nx, ny)):
            for which in (0, 1):
                if d < (nx, ny)[which if make is first else 1 - which]:
                    act(make(which, z_, d))

    def start(cp):
        cp.start()

    def arrived(cp):
        cp.wait_recv()

    def sent(cp):
        cp.wait_send()

    def send_enc_right(j, r):
        ref = enc.at[j, pl.ds(r * rows, rows)]
        return copy(ref, ref, esr.at[j, r], err.at[j, r], right)

    def send_enc_left(j, r):
        ref = enc.at[j, pl.ds(r * rows, rows)]
        return copy(ref, ref, esl.at[j, r], erl.at[j, r], left)

    def send_valid():
        return copy(valid.at[1], valid.at[0], vs.at[0], vr.at[0], (s + 1, h))

    other = 1 - zh

    def weights_a():
        each(first, zh, start)
        for i in (0, 1):
            cross_up(i, 0).start()

    def weights_b():
        for i in (0, 1):
            cross_up(i, 0).wait_recv()
            cross_up(i, 1).start()
        each(first, zh, arrived)
        each(second, zh, start)

    def weights_c():
        for i in (0, 1):
            cross_up(i, 1).wait_recv()
        each(first, other, start)

    def weights_d():
        each(second, zh, arrived)
        share(zh).start()
        each(first, other, arrived)
        each(second, other, start)

    def weights_e():
        each(second, other, arrived)
        share(other).start()

    weights_a()

    @when(has_next)
    def _():
        send_valid().start()

    todo = {1: weights_b, 2: weights_c, 3: weights_d, 5: weights_e}
    steps = nz - 1
    for st in range(nz):
        for r in range(CHUNKS):
            if st > 0:

                @when(h - st >= 0)
                def _():
                    send_enc_right(h - st, r).wait_recv()

            if st < steps:

                @when(h - st >= 0, h < nz - 1)
                def _():
                    send_enc_right(h - st, r).start()

            if st > 0:

                @when(h + st < nz)
                def _():
                    send_enc_left(h + st, r).wait_recv()

            if st < steps:

                @when(h + st < nz, h > 0)
                def _():
                    send_enc_left(h + st, r).start()

        if st in todo:
            todo[st]()
    for st in sorted(todo):
        if st >= nz:
            todo[st]()
    share(zh).wait_recv()
    share(other).wait_recv()

    proj[...] = jnp.zeros_like(proj)

    def project(f, carry):
        block = w[f // nh, f % nh].reshape(-1, 2 * width)
        proj[...] += dot(enc[f], block, 1, 0)
        return carry

    lax.fori_loop(0, nz, project, 0)
    kv[1] = proj[...].astype(BF)

    def kv_direct():
        return copy(kv.at[1], kv.at[0], ks.at[0], kr.at[0], (s + 1, h))

    def kv_part(i):
        return copy(kv.at[1, pl.ds(i * piece, piece)], ra, ps.at[i], pr.at[0], (at(x, zh, i, nc - 1), h))

    def crossing(src, mid, dst, ss, rs, i, leg):
        cols, dev = (KC, up) if i == 0 else (VC, down)
        a, b = (src, mid) if leg == 0 else (mid, dst)
        return copy(a.at[:, cols], b.at[:, cols], ss.at[i, leg], rs.at[i, leg], dev)

    def cross_all(src, mid, dst, ss, rs):
        for i in (0, 1):
            crossing(src, mid, dst, ss, rs, i, 0).start()
        for i in (0, 1):
            crossing(src, mid, dst, ss, rs, i, 0).wait_recv()
            crossing(src, mid, dst, ss, rs, i, 1).start()
        for i in (0, 1):
            crossing(src, mid, dst, ss, rs, i, 1).wait_recv()

    def kv_final():
        return copy(rc, kv.at[0, pl.ds(pl.multiple_of(y * piece, piece), piece)], fs.at[0], fr.at[y], (at(served_x, zh, 0, 0), h))

    @when(has_next, jnp.logical_not(far_next))
    def _():
        kv_direct().start()

    @when(far_next)
    def _():
        for i in range(ny - 1):
            kv_part(i).start()
        ra[...] = kv[1, (ny - 1) * piece :]

    @when(relay)
    def _():
        @when(y < ny - 1)
        def _():
            kv_part(0).wait_recv()

        cross_all(ra, rm, rc, cs, cr)

        @when(serves)
        def _():
            kv_final().start()

    @when(has_prev)
    def _():
        send_valid().wait_recv()

        @when(jnp.logical_not(far_prev))
        def _():
            kv_direct().wait_recv()

        @when(far_prev)
        def _():
            for i in range(ny):
                copy(rc, kv.at[0, pl.ds(i * piece, piece)], fs.at[0], fr.at[i], sib).wait_recv()

    scale = 1.0 / math.sqrt(HD)
    own = lax.broadcasted_iota(jnp.int32, (tokens, lmax), 0) >= off_ref[0]
    ok = jnp.where(own, valid[1, 0:1, :], valid[0, 0:1, :]) > 0.5
    for a in range(heads):
        kc = slice(a * HD, (a + 1) * HD)
        vc = slice(width + a * HD, width + (a + 1) * HD)
        q = q_ref[:, kc]
        g = g_ref[:, kc]
        k = kv[:, :, kc].reshape(2 * lmax, HD)
        v = kv[:, :, vc].reshape(2 * lmax, HD)
        both = dot(q, k, 1, 1)
        scores = jnp.where(own, both[:, lmax:], both[:, :lmax]) * scale
        scores = jnp.where(ok, scores, -1e30)
        expo = jnp.exp(scores - jnp.max(scores, axis=-1, keepdims=True))
        probs = expo / jnp.sum(expo, axis=-1, keepdims=True)
        both = dot(g, v, 1, 1)
        dprobs = jnp.where(own, both[:, lmax:], both[:, :lmax])
        delta = jnp.sum(probs * dprobs, axis=-1, keepdims=True)
        ds = probs * (dprobs - delta) * scale
        pc = jnp.concatenate([jnp.where(own, 0.0, probs), jnp.where(own, probs, 0.0)], axis=1).astype(BF)
        dc = jnp.concatenate([jnp.where(own, 0.0, ds), jnp.where(own, ds, 0.0)], axis=1).astype(BF)
        out_ref[:, kc] = dot(pc, v, 1, 0).astype(BF)
        dq_ref[:, kc] = dot(dc, k, 1, 0).astype(BF)
        dk = dot(dc, q, 0, 0)
        dv = dot(pc, g, 0, 0)
        dprev[:, kc] = dk[:lmax].astype(BF)
        dprev[:, vc] = dv[:lmax].astype(BF)
        dk32[:, kc] = dk[lmax:]
        dk32[:, vc] = dv[lmax:]

    def back_direct():
        return copy(dprev, dback, bks.at[0], bkr.at[0], (s - 1, h))

    def back_part(i):
        return copy(dprev.at[pl.ds(i * piece, piece)], ba, bps.at[i], bpr.at[0], (at(source_x, zh, i, nc - 1), h))

    def back_final():
        return copy(bc, dback.at[pl.ds(pl.multiple_of(y * piece, piece), piece)], bfs.at[0], bfr.at[y], (at(x, zh, ny - 1, nc - 1), h))

    @when(has_prev, jnp.logical_not(far_prev))
    def _():
        back_direct().start()

    @when(has_prev, far_prev)
    def _():
        for i in range(ny):
            back_part(i).start()

    @when(relay)
    def _():
        @when(serves)
        def _():
            back_part(0).wait_recv()

        @when(jnp.logical_not(serves))
        def _():
            ba[...] = jnp.zeros_like(ba)

        cross_all(ba, bm, bc, bcs, bcr)

        @when(goes, y < ny - 1)
        def _():
            back_final().start()

        @when(goes, y == ny - 1)
        def _():
            dback[(ny - 1) * piece :, :] = bc[...]

    @when(has_next)
    def _():
        @when(jnp.logical_not(far_next))
        def _():
            back_direct().wait_recv()

        @when(far_next)
        def _():
            for i in range(ny - 1):
                copy(bc, dback.at[pl.ds(i * piece, piece)], bfs.at[0], bfr.at[i], sib).wait_recv()

    dkv[...] = (dk32[...] + dback[...].astype(F32)).astype(BF)

    def sum_right(j, r):
        ref = rr.at[j, pl.ds(r * rows, rows)]
        return copy(ref, ref, rsr.at[j, r], rrr.at[j, r], right)

    def sum_left(j, r):
        ref = rl.at[j, pl.ds(r * rows, rows)]
        return copy(ref, ref, rsl.at[j, r], rrl.at[j, r], left)

    def partial(j, r):
        block = w[j // nh, j % nh].reshape(-1, 2 * width)
        return dot(dkv[pl.ds(r * rows, rows), :], block, 1, 1)

    def reduce_step(t, carry):
        for r in range(CHUNKS):
            here = pl.ds(r * rows, rows)

            @when(t >= h, h < nz - 1)
            def _():
                j = nz - 1 + h - t
                part = partial(j, r)

                @when(h > 0)
                def _():
                    sum_right(j, r).wait_recv()

                rr[j, here, :] = (part + rr[j, here, :].astype(F32)).astype(BF)
                sum_right(j, r).start()

            @when(t >= nz - 1 - h, h > 0)
            def _():
                j = t - (nz - 1 - h)
                part = partial(j, r)

                @when(h < nz - 1)
                def _():
                    sum_left(j, r).wait_recv()

                rl[j, here, :] = (part + rl[j, here, :].astype(F32)).astype(BF)
                sum_left(j, r).start()

        return carry

    lax.fori_loop(0, nz - 1, reduce_step, 0)

    for r in range(CHUNKS):
        here = pl.ds(r * rows, rows)
        part = partial(h, r)

        @when(h > 0)
        def _():
            sum_right(h, r).wait_recv()

        @when(h < nz - 1)
        def _():
            sum_left(h, r).wait_recv()

        total = part + rr[h, here, :].astype(F32) + rl[h, here, :].astype(F32)
        de_ref[0, here, :] = total.astype(BF)

    each(first, 0, sent)
    each(first, 1, sent)
    each(second, 0, sent)
    each(second, 1, sent)
    share(0).wait_send()
    share(1).wait_send()
    for i in (0, 1):
        for leg in (0, 1):
            cross_up(i, leg).wait_send()

    @when(has_next)
    def _():
        send_valid().wait_send()

    @when(has_next, jnp.logical_not(far_next))
    def _():
        kv_direct().wait_send()

    @when(far_next)
    def _():
        for i in range(ny - 1):
            kv_part(i).wait_send()

    @when(has_prev, jnp.logical_not(far_prev))
    def _():
        back_direct().wait_send()

    @when(has_prev, far_prev)
    def _():
        for i in range(ny):
            back_part(i).wait_send()

    @when(relay)
    def _():
        for i in (0, 1):
            for leg in (0, 1):
                crossing(ra, rm, rc, cs, cr, i, leg).wait_send()
                crossing(ba, bm, bc, bcs, bcr, i, leg).wait_send()

        @when(serves)
        def _():
            kv_final().wait_send()

        @when(goes, y < ny - 1)
        def _():
            back_final().wait_send()

    def drain(j, carry):
        for r in range(CHUNKS):

            @when(j <= h, h < nz - 1)
            def _():
                send_enc_right(j, r).wait_send()

            @when(j >= h, h > 0)
            def _():
                send_enc_left(j, r).wait_send()

            @when(j > h)
            def _():
                sum_right(j, r).wait_send()

            @when(j < h)
            def _():
                sum_left(j, r).wait_send()

        return carry

    lax.fori_loop(0, nz, drain, 0)


def shards(nz, queries, encodings, key_weight, value_weight, text_length, image_offset, cotangent):
    nx, nh, ny, nc = GRID
    tokens, width = queries.shape
    _, lmax, feat = encodings.shape
    depth = key_weight.shape[0]
    assert nx * nh == nz and ny * nc * depth == feat
    piece = lmax // ny
    dma = pltpu.SemaphoreType.DMA
    vmem = pl.BlockSpec(memory_space=pltpu.VMEM)
    smem = pl.BlockSpec(memory_space=pltpu.SMEM)
    part = pltpu.VMEM((piece, 2 * width), BF)
    whole = pltpu.VMEM((lmax, 2 * width), BF)
    far = max(nx, ny) - 1
    scratch = [
        pltpu.VMEM((nx, nh, ny, nc, depth, 2 * width), BF),
        pltpu.VMEM((depth, 2 * width), BF),
        pltpu.VMEM((nz, lmax, feat), BF),
        pltpu.VMEM((2, lmax, 2 * width), BF),
        pltpu.VMEM((2, 8, lmax), F32),
        part, part, part, part, part, part,
        pltpu.VMEM((lmax, 2 * width), F32),
        whole, whole, whole,
        pltpu.VMEM((nz, lmax, feat), BF),
        pltpu.VMEM((nz, lmax, feat), BF),
        pltpu.VMEM((lmax, 2 * width), F32),
        dma((2, far, nh)), dma((2, far, nh)), dma((2, far, nh)), dma((2, far, nh)),
        dma((4,)), dma((4,)), dma((nh,)), dma((nh,)),
        dma((nz, CHUNKS)), dma((nz, CHUNKS)), dma((nz, CHUNKS)), dma((nz, CHUNKS)),
        dma((1,)), dma((1,)),
        dma((1,)), dma((1,)), dma((ny,)), dma((1,)), dma((2, 2)), dma((2, 2)), dma((1,)), dma((ny,)),
        dma((1,)), dma((1,)), dma((ny,)), dma((1,)), dma((2, 2)), dma((2, 2)), dma((1,)), dma((ny,)),
        dma((nz, CHUNKS)), dma((nz, CHUNKS)), dma((nz, CHUNKS)), dma((nz, CHUNKS)),
    ]
    return pl.pallas_call(
        functools.partial(kernel, (nx, nh, ny, nc, nz)),
        out_shape=(
            jax.ShapeDtypeStruct(queries.shape, BF),
            jax.ShapeDtypeStruct(queries.shape, BF),
            jax.ShapeDtypeStruct(encodings.shape, BF),
        ),
        in_specs=[smem, smem] + [vmem] * 5,
        out_specs=(vmem, vmem, vmem),
        scratch_shapes=scratch,
        compiler_params=pltpu.CompilerParams(
            collective_id=0, has_side_effects=True, vmem_limit_bytes=56 * 2**20
        ),
        name="flow_block",
    )(text_length, image_offset, queries, cotangent, encodings, key_weight, value_weight)


def solution(mesh):
    return jax.shard_map(
        functools.partial(shards, mesh.shape["head"]),
        mesh=mesh,
        in_specs=(
            P("seq", "head"),
            P("seq", None, "head"),
            P("seq", "head"),
            P("seq", "head"),
            P("seq"),
            P("seq"),
            P("seq", "head"),
        ),
        out_specs=(P("seq", "head"), P("seq", "head"), P("seq", None, "head")),
        check_vma=False,
    )
```

time: 484 us -> 147 us (0.30)
  the two profiles are of different devices: /device:TPU:24 before, /device:TPU:49 now
where the time goes in v1:
time: 147 us; the launch traced here: 146 us
  Pallas kernels  141 us (96%)
  local copies, waits for them, and re-layouts  3.63 us (2%)
  between operations  1.94 us (1%)
    pallas_call x1, Pallas kernels, shards(): pl.pallas_call(functools.partial(kernel, (nx, nh, ny, nc, nz)), out_shape...  141 us
    unnamed x7, local copies, waits for them, and re-layouts  3.63 us

profile of v1, /device:TPU:49, one launch (start us, length us, event | category | flops | bytes accessed | tf_op | source)
XLA Modules:
  0.0 146.5 jit_solution(7615039202114827737)
XLA Ops:
  1.9 140.9 %flow_block.1 = (bf16[512,384]{1,0:T(8,128)(2,1)}, bf16[512,384]{1,0:T(8,128)(2,1)}, bf16[1,256,512]{2,1,0:T(8,128)(2,1)}) custom-call(s32[1]{0:T(128)S(6)} %copy.13.len_ref, s32[1]{0:T(128)S(6)} %copy.14.off_ref, bf16[512,384]{1,0:T(8,128)(2,1)} %q_ref.1, bf16[512,384]{1,0:T(8,128)(2,1)} %g_ref.1, bf16[1,256,512]{2,1,0:T(8,128)(2,1)} %enc_ref.1, ...), custom_call_target="tpu_custom_call" | custom-call | tf_op jit(solution)/shard_map/flow_block/pallas_call | solution.py:581
  142.8 0.0 copy-start
  142.9 1.8 %copy.15 = bf16[512,384]{1,0:T(8,128)(2,1)} copy(bf16[512,384]{1,0:T(8,128)(2,1)} %get-tuple-element.6) | data formatting | bytes 786432
  144.7 0.0 copy-done
  144.7 0.0 copy-start.1
  144.7 0.7 copy.16
  145.4 0.3 copy-done.1
  145.8 0.7 copy.17
Async XLA Ops:
  142.8 1.8 %copy-start = (bf16[512,384]{1,0:T(8,128)(2,1)S(1)}, bf16[512,384]{1,0:T(8,128)(2,1)}, u32[]{:S(2)}) copy-start(bf16[512,384]{1,0:T(8,128)(2,1)} %get-tuple-element.7) | copy-start | bytes 1179652
  144.7 1.1 copy-start.1

commit v2 on v0

v2 whole, which is shorter than its diff:
```python
import functools
import math

import jax
import jax.numpy as jnp
from jax import lax
from jax.experimental import pallas as pl
from jax.experimental.pallas import tpu as pltpu
from jax.sharding import PartitionSpec as P

HD = 128
GRID = (4, 2, 4, 2)
CHUNKS = 4
BF = jnp.bfloat16
F32 = jnp.float32
MESH = pl.DeviceIdType.MESH


def dot(a, b, da, db):
    return lax.dot_general(a, b, (((da,), (db,)), ((), ())), preferred_element_type=F32)


def kernel(
    dims, len_ref, off_ref, q_ref, g_ref, enc_ref, wk_ref, wv_ref,
    out_ref, dq_ref, de_ref,
    w, wmid, enc, kv, qg, qp, ro, rn, rp, ra, rm, rc, ba, bm, bc, dkv32, dkv, rr, rl, parts,
    wss, wrs, wsx, wrx, wsb, wrb, wso, wro, gate,
    esr, err, esl, erl,
    ks, kr, ps, pr, cs, cr, fs, fr,
    bks, bkr, bps, bpr, bcs, bcr, bfs, bfr,
    rsr, rrr, rsl, rrl,
):
    nx, nh, ny, nc, nz = dims
    width = wk_ref.shape[1]
    heads = width // HD
    lmax = enc_ref.shape[1]
    tokens = q_ref.shape[0]
    piece = tokens // ny
    rows = lmax // CHUNKS
    s = lax.axis_index("seq")
    h = lax.axis_index("head")
    c = s % nc
    y = (s // nc) % ny
    zh = (s // (nc * ny)) % nh
    x = s // (nc * ny * nh)
    last = nx * nh * ny * nc - 1

    def at(x_, zh_, y_, c_):
        return ((x_ * nh + zh_) * ny + y_) * nc + c_

    def along(steps):
        z = (zh * nz + h + steps + nh * nz) % (nh * nz)
        return (at(x, z // nz, y, c), z % nz), z // nz

    sib = (at(x, zh, y, 1 - c), h)
    up, zh_up = along(nz // 2)
    down, zh_down = along(-(nz // 2))
    place = ((x, nx), (y, ny))

    def beside(axis, way):
        here, size = place[axis]
        there = (here + way + size) % size
        return there, ((at(there, zh, y, c) if axis == 0 else at(x, zh, there, c)), h)

    right = (s, h + 1)
    left = (s, h - 1)
    KC, VC = slice(0, width), slice(width, 2 * width)

    has_next = s < last
    has_prev = s > 0
    far_next = jnp.logical_and(c == nc - 1, y == ny - 1)
    far_prev = jnp.logical_and(c == 0, y == 0)
    near_next = jnp.logical_and(c == nc - 1, y < ny - 1)
    near_prev = jnp.logical_and(c == 0, y > 0)
    first_core = c == 0
    second_core = c == nc - 1
    serves = jnp.logical_or(zh == 1, x < nx - 1)
    served = (at(jnp.where(zh == 1, x, x + 1), zh, 0, 0), h)
    itself = jnp.logical_and(zh == 1, jnp.logical_and(first_core, y == 0))
    goes = jnp.logical_not(jnp.logical_and(zh == 1, x == nx - 1))
    source = (at(x, zh, ny - 1, nc - 1), h)
    source_x = jnp.where(zh == 1, x, x - 1)

    def when(*conds):
        return pl.when(functools.reduce(jnp.logical_and, conds))

    def copy(src, dst, ss, rs, dev):
        return pltpu.make_async_remote_copy(
            src_ref=src, dst_ref=dst, send_sem=ss, recv_sem=rs, device_id=dev, device_id_type=MESH
        )

    barrier = pltpu.get_barrier_semaphore()

    def hello(dev):
        pl.semaphore_signal(barrier, inc=1, device_id=dev, device_id_type=MESH)

    hello(sib)
    hello(up)
    hello(down)

    @when(h < nz - 1)
    def _():
        hello(right)

    @when(h > 0)
    def _():
        hello(left)

    @when(near_next)
    def _():
        hello((s + 1, h))

    @when(near_prev)
    def _():
        hello((s - 1, h))

    @when(first_core)
    def _():
        for axis in (0, 1):
            for way in (1, -1):
                hello(beside(axis, way)[1])

    @when(serves, jnp.logical_not(itself))
    def _():
        hello(served)

    beside_source = jnp.logical_and(goes, jnp.logical_not(far_next))

    @when(beside_source)
    def _():
        hello(source)

    far_target = jnp.logical_and(far_prev, has_prev)
    far_source = jnp.logical_and(far_next, has_next)

    @when(far_target)
    def _():
        for i in range(ny):
            hello((at(source_x, zh, i, nc - 1), h))
            if i > 0:
                hello((at(source_x, zh, i, 0), h))

        @when(zh == 0)
        def _():
            hello((at(source_x, zh, 0, 0), h))

    @when(far_source)
    def _():
        for i in range(ny):
            hello((at(x, zh, i, 0), h))
            if i < ny - 1:
                hello((at(x, zh, i, nc - 1), h))

    @when(first_core)
    def _():
        w[x, zh, y, 0, :, KC] = wk_ref[...]
        w[x, zh, y, 0, :, VC] = wv_ref[...]

    @when(second_core)
    def _():
        wmid[0, :, KC] = wk_ref[...]
        wmid[0, :, VC] = wv_ref[...]

    enc[h] = enc_ref[0]
    own = lax.broadcasted_iota(jnp.int32, (tokens, width), 0) >= off_ref[0]
    for cols, ref in ((KC, q_ref), (VC, g_ref)):
        block = ref[...].astype(F32)
        qg[1, :, cols] = jnp.where(own, block, 0.0).astype(BF)
        qp[:, cols] = jnp.where(own, 0.0, block).astype(BF)

    @when(s == 0)
    def _():
        rp[...] = jnp.zeros_like(rp)

    @when(s == last)
    def _():
        qg[0] = jnp.zeros((tokens, 2 * width), BF)

    @when(h == 0)
    def _():
        rr[...] = jnp.zeros_like(rr)

    @when(h == nz - 1)
    def _():
        rl[...] = jnp.zeros_like(rl)

    @when(first_core, jnp.logical_not(serves))
    def _():
        ba[...] = jnp.zeros_like(ba)

    @when(second_core, jnp.logical_not(goes))
    def _():
        ra[...] = jnp.zeros_like(ra)

    def n(flag):
        return flag.astype(jnp.int32)

    count = 3 + n(h < nz - 1) + n(h > 0) + n(near_next) + n(near_prev) + 4 * n(first_core)
    count = count + n(jnp.logical_and(serves, jnp.logical_not(itself))) + n(beside_source)
    count = count + n(far_target) * (2 * ny - 1 + n(zh == 0)) + n(far_source) * (2 * ny - 1)
    pl.semaphore_wait(barrier, count)

    def lend():
        return copy(wmid.at[0], w.at[x, zh, y, nc - 1], wso.at[0], wro.at[0], sib)

    def cross(i, leg):
        cols, dev, z_ = (KC, up, zh_down) if i == 0 else (VC, down, zh_up)
        mid = wmid.at[:, :, cols]
        if leg == 0:
            return copy(w.at[x, zh, y, :, :, cols], mid, wsx.at[2 * i], wrx.at[2 * i], dev)
        return copy(mid, w.at[x, z_, y, :, :, cols], wsx.at[2 * i + 1], wrx.at[2 * i + 1], dev)

    def hop(stage, which, z_, k):
        axis = which if stage == 0 else 1 - which
        index = place[axis][0] if k < 2 else beside(axis, -1 if k == 2 else 1)[0]
        dev = beside(axis, 1 if k % 2 == 0 else -1)[1]
        cols = KC if which == 0 else VC
        core = slice(None) if k < 2 else k - 2
        if axis == 0:
            ref = w.at[index, z_, y, core, :, cols] if stage == 0 else w.at[index, z_, :, core, :, cols]
        else:
            ref = w.at[x, z_, index, core, :, cols] if stage == 0 else w.at[:, z_, index, core, :, cols]
        return copy(ref, ref, wss.at[stage, which, z_, k], wrs.at[stage, which, z_, k], dev)

    def share(which, z_, d):
        here, size = place[1 - which]
        index = (here + d) % size
        ref = w.at[:, z_, index, :, :, KC] if which == 0 else w.at[index, z_, :, :, :, VC]
        return copy(ref, ref, wsb.at[which, z_, d], wrb.at[which, z_, d], sib)

    def send(stage, z_, ks_):
        for which in (0, 1):
            for k in ks_:
                hop(stage, which, z_, k).start()

    def receive(stage, z_, ks_):
        for which in (0, 1):
            for k in ks_:
                hop(stage, which, z_, k).wait_recv()

    def shares(z_, ds, act):
        for which in (0, 1):
            for d in ds:
                act(share(which, z_, d))

    def start(cp):
        cp.start()

    other = 1 - zh

    def task_a():
        lend().wait_recv()
        for i in (0, 1):
            cross(i, 0).start()
        send(0, zh, (0, 1))

    def task_b():
        receive(0, zh, (0, 1))
        send(0, zh, (2, 3))

    def task_c():
        for i in (0, 1):
            cross(i, 0).wait_recv()
            cross(i, 1).start()

    def task_d():
        receive(0, zh, (2, 3))
        send(1, zh, (0, 1))

    def task_e():
        for i in (0, 1):
            cross(i, 1).wait_recv()
        send(0, other, (0, 1))

    def task_f():
        receive(0, other, (0, 1))
        send(0, other, (2, 3))

    def task_g():
        receive(1, zh, (0, 1))
        send(1, zh, (2, 3))
        shares(zh, (0, 1, 3), start)

    def task_h():
        receive(0, other, (2, 3))
        send(1, other, (0, 1))

    def task_i():
        receive(1, zh, (2, 3))
        shares(zh, (2,), start)

    def task_j():
        receive(1, other, (0, 1))
        send(1, other, (2, 3))
        shares(other, (0, 1, 3), start)

    def task_k():
        receive(1, other, (2, 3))
        shares(other, (2,), start)

    def crossing(src, mid, dst, ss, rs, i, leg):
        cols, dev = (KC, up) if i == 0 else (VC, down)
        a, b = (src, mid) if leg == 0 else (mid, dst)
        return copy(a.at[:, cols], b.at[:, cols], ss.at[i, leg], rs.at[i, leg], dev)

    def back_crossing(i, leg):
        return crossing(ba, bm, bc, bcs, bcr, i, leg)

    def there_crossing(i, leg):
        return crossing(ra, rm, rc, cs, cr, i, leg)

    def back_direct():
        return copy(qp, qg.at[0], bks.at[0], bkr.at[0], (s - 1, h))

    def back_part(i):
        return copy(qp.at[pl.ds(i * piece, piece)], ba, bps.at[i], bpr.at[0], (at(source_x, zh, i, 0), h))

    def back_final(i):
        return copy(bc, qg.at[0, pl.ds(i * piece, piece)], bfs.at[0], bfr.at[i], source)

    def back_start():
        @when(has_prev, jnp.logical_not(far_prev))
        def _():
            back_direct().start()

        @when(far_target)
        def _():
            for i in range(1, ny):
                back_part(i).start()

            @when(zh == 0)
            def _():
                back_part(0).start()

            @when(zh == 1)
            def _():
                ba[...] = qp[:piece, :]

    def back_one():
        @when(serves, jnp.logical_not(itself))
        def _():
            back_part(0).wait_recv()

        for i in (0, 1):
            back_crossing(i, 0).start()

    def back_two():
        for i in (0, 1):
            back_crossing(i, 0).wait_recv()
            back_crossing(i, 1).start()

    def back_three():
        for i in (0, 1):
            back_crossing(i, 1).wait_recv()
        for i in range(ny):

            @when(goes, y == i)
            def _():
                back_final(i).start()

    def back_arrived():
        @when(has_next)
        def _():
            @when(jnp.logical_not(far_next))
            def _():
                back_direct().wait_recv()

            @when(far_next)
            def _():
                for i in range(ny):
                    back_final(i).wait_recv()

    def send_enc_right(j, r):
        ref = enc.at[j, pl.ds(r * rows, rows)]
        return copy(ref, ref, esr.at[j, r], err.at[j, r], right)

    def send_enc_left(j, r):
        ref = enc.at[j, pl.ds(r * rows, rows)]
        return copy(ref, ref, esl.at[j, r], erl.at[j, r], left)

    def project(f):
        if nx * nh == nz:
            block = w[f // nh, f % nh].reshape(-1, 2 * width)
        else:
            block = w[f].reshape(-1, 2 * width)
        return dot(enc[f], block, 1, 0)

    def gather(todo, projecting):
        for st in range(nz):
            for r in range(CHUNKS):
                if st > 0:

                    @when(h - st >= 0)
                    def _():
                        send_enc_right(h - st, r).wait_recv()

                if st < nz - 1:

                    @when(h - st >= 0, h < nz - 1)
                    def _():
                        send_enc_right(h - st, r).start()

                if st > 0:

                    @when(h + st < nz)
                    def _():
                        send_enc_left(h + st, r).wait_recv()

                if st < nz - 1:

                    @when(h + st < nz, h > 0)
                    def _():
                        send_enc_left(h + st, r).start()

            for task in todo.get(st, ()):
                task()
            if projecting:
                for d in {nz - 4: (0, 1), nz - 3: (2, 3), nz - 2: (4, 5), nz - 1: (6, 7)}.get(st, ()):
                    if d == 0:
                        dkv32[...] = project(h)
                    else:

                        @when(h - d >= 0)
                        def _():
                            dkv32[...] += project(h - d)

                        @when(h + d < nz)
                        def _():
                            dkv32[...] += project(h + d)

    back_start()

    @when(second_core)
    def _():
        lend().start()
        gather({}, False)
        pl.semaphore_signal(gate, inc=1, device_id=sib, device_id_type=MESH)
        for z_ in (0, 1):
            for which in (0, 1):
                for d in range(4):
                    share(which, z_, d).wait_recv()
        dkv32[...] = jnp.zeros_like(dkv32)

        def one(f, carry):
            dkv32[...] += project(f)
            return carry

        lax.fori_loop(0, nz, one, 0)

    @when(first_core)
    def _():
        for task in (
            task_a, task_b, back_one, task_c, task_d, task_e, back_two, task_f, task_g, task_h, task_i, back_three,
        ):
            task()
        pl.semaphore_wait(gate, 1)
        gather({1: (task_j,), 2: (task_k,)}, True)

    kv[...] = dkv32[...].astype(BF)

    scale = 1.0 / math.sqrt(HD)
    ok = lax.broadcasted_iota(jnp.int32, (1, lmax), 1) < len_ref[0]
    for b in (1, 0):
        if b == 0:
            back_arrived()
        result = ro if b == 1 else rn
        for a in range(heads):
            kc = slice(a * HD, (a + 1) * HD)
            vc = slice(width + a * HD, width + (a + 1) * HD)
            q = qg[b, :, kc]
            g = qg[b, :, vc]
            k = kv[:, kc]
            v = kv[:, vc]
            scores = jnp.where(ok, dot(q, k, 1, 1) * scale, -1e30)
            expo = jnp.exp(scores - jnp.max(scores, axis=-1, keepdims=True))
            probs = expo / jnp.sum(expo, axis=-1, keepdims=True)
            dprobs = dot(g, v, 1, 1)
            delta = jnp.sum(probs * dprobs, axis=-1, keepdims=True)
            ds = (probs * (dprobs - delta) * scale).astype(BF)
            pb = probs.astype(BF)
            result[:, kc] = dot(pb, v, 1, 0).astype(BF)
            result[:, vc] = dot(ds, k, 1, 0).astype(BF)
            dk = dot(ds, q, 0, 0)
            dv = dot(pb, g, 0, 0)
            if b == 1:
                dkv32[:, kc] = dk
                dkv32[:, vc] = dv
            else:
                dkv[:, kc] = (dkv32[:, kc] + dk).astype(BF)
                dkv[:, vc] = (dkv32[:, vc] + dv).astype(BF)

    def there_direct():
        return copy(rn, rp, ks.at[0], kr.at[0], (s + 1, h))

    def there_part(i):
        return copy(rn.at[pl.ds(i * piece, piece)], ra, ps.at[i], pr.at[0], (at(x, zh, i, nc - 1), h))

    def there_final(i):
        return copy(rc, rp.at[pl.ds(i * piece, piece)], fs.at[0], fr.at[i], served)

    def there_one():
        @when(goes, y < ny - 1)
        def _():
            there_part(0).wait_recv()

        for i in (0, 1):
            there_crossing(i, 0).start()

    def there_two():
        for i in (0, 1):
            there_crossing(i, 0).wait_recv()
            there_crossing(i, 1).start()

    def there_three():
        for i in (0, 1):
            there_crossing(i, 1).wait_recv()
        for i in range(ny):

            @when(serves, y == i)
            def _():
                there_final(i).start()

    @when(has_next, jnp.logical_not(far_next))
    def _():
        there_direct().start()

    @when(far_source)
    def _():
        for i in range(ny - 1):
            there_part(i).start()
        ra[...] = rn[(ny - 1) * piece :, :]

    def sum_right(j, r):
        ref = rr.at[j, pl.ds(r * rows, rows)]
        return copy(ref, ref, rsr.at[j, r], rrr.at[j, r], right)

    def sum_left(j, r):
        ref = rl.at[j, pl.ds(r * rows, rows)]
        return copy(ref, ref, rsl.at[j, r], rrl.at[j, r], left)

    def partial(j):
        if nx * nh == nz:
            block = w[j // nh, j % nh].reshape(-1, 2 * width)
        else:
            block = w[j].reshape(-1, 2 * width)
        return dot(dkv[...], block, 1, 1)

    def reduce_step(t, carry):
        going_right = jnp.logical_and(t >= h, h < nz - 1)
        going_left = jnp.logical_and(t >= nz - 1 - h, h > 0)
        jr = nz - 1 + h - t
        jl = t - (nz - 1 - h)

        @when(going_right)
        def _():
            parts[0] = partial(jr)

        @when(going_left)
        def _():
            parts[1] = partial(jl)

        for r in range(CHUNKS):
            here = pl.ds(r * rows, rows)

            @when(going_right)
            def _():
                @when(h > 0)
                def _():
                    sum_right(jr, r).wait_recv()

                rr[jr, here, :] = (parts[0, here, :] + rr[jr, here, :].astype(F32)).astype(BF)
                sum_right(jr, r).start()

            @when(going_left)
            def _():
                @when(h < nz - 1)
                def _():
                    sum_left(jl, r).wait_recv()

                rl[jl, here, :] = (parts[1, here, :] + rl[jl, here, :].astype(F32)).astype(BF)
                sum_left(jl, r).start()

        @when(second_core, t == nz // 2)
        def _():
            there_one()

        return carry

    lax.fori_loop(0, nz - 1, reduce_step, 0)

    @when(second_core)
    def _():
        there_two()

    parts[0] = partial(h)
    for r in range(CHUNKS):
        here = pl.ds(r * rows, rows)

        @when(h > 0)
        def _():
            sum_right(h, r).wait_recv()

        @when(h < nz - 1)
        def _():
            sum_left(h, r).wait_recv()

        total = parts[0, here, :] + rr[h, here, :].astype(F32) + rl[h, here, :].astype(F32)
        de_ref[0, here, :] = total.astype(BF)

    @when(second_core)
    def _():
        there_three()

    @when(has_prev)
    def _():
        @when(jnp.logical_not(far_prev))
        def _():
            there_direct().wait_recv()

        @when(far_prev)
        def _():
            for i in range(ny):
                there_final(i).wait_recv()

    own = lax.broadcasted_iota(jnp.int32, (tokens, width), 0) >= off_ref[0]
    for cols, ref in ((KC, out_ref), (VC, dq_ref)):
        ref[...] = jnp.where(own, ro[:, cols].astype(F32), rp[:, cols].astype(F32)).astype(BF)

    @when(first_core)
    def _():
        for z_ in (0, 1):
            for which in (0, 1):
                for d in range(4):
                    share(which, z_, d).wait_send()
                    for stage in (0, 1):
                        hop(stage, which, z_, d).wait_send()
        for i in (0, 1):
            for leg in (0, 1):
                cross(i, leg).wait_send()
                back_crossing(i, leg).wait_send()

        @when(goes)
        def _():
            back_final(0).wait_send()

    @when(second_core)
    def _():
        lend().wait_send()
        for i in (0, 1):
            for leg in (0, 1):
                there_crossing(i, leg).wait_send()

        @when(serves)
        def _():
            there_final(0).wait_send()

    @when(has_prev, jnp.logical_not(far_prev))
    def _():
        back_direct().wait_send()

    @when(far_target)
    def _():
        for i in range(1, ny):
            back_part(i).wait_send()

        @when(zh == 0)
        def _():
            back_part(0).wait_send()

    @when(has_next, jnp.logical_not(far_next))
    def _():
        there_direct().wait_send()

    @when(far_source)
    def _():
        for i in range(ny - 1):
            there_part(i).wait_send()

    def drain(j, carry):
        for r in range(CHUNKS):

            @when(j <= h, h < nz - 1)
            def _():
                send_enc_right(j, r).wait_send()

            @when(j >= h, h > 0)
            def _():
                send_enc_left(j, r).wait_send()

            @when(j > h)
            def _():
                sum_right(j, r).wait_send()

            @when(j < h)
            def _():
                sum_left(j, r).wait_send()

        return carry

    lax.fori_loop(0, nz, drain, 0)


def shards(nz, queries, encodings, key_weight, value_weight, text_length, image_offset, cotangent):
    nx, nh, ny, nc = GRID
    tokens, width = queries.shape
    _, lmax, feat = encodings.shape
    depth = key_weight.shape[0]
    assert ny * nc * depth * nx * nh == feat * nz
    dma = pltpu.SemaphoreType.DMA
    vmem = pl.BlockSpec(memory_space=pltpu.VMEM)
    smem = pl.BlockSpec(memory_space=pltpu.SMEM)
    block = pltpu.VMEM((tokens, 2 * width), BF)
    part = pltpu.VMEM((tokens // ny, 2 * width), BF)
    line = dma((nz, CHUNKS))
    scratch = [
        pltpu.VMEM((nx, nh, ny, nc, depth, 2 * width), BF),
        pltpu.VMEM((nc, depth, 2 * width), BF),
        pltpu.VMEM((nz, lmax, feat), BF),
        pltpu.VMEM((lmax, 2 * width), BF),
        pltpu.VMEM((2, tokens, 2 * width), BF),
        block, block, block, block,
        part, part, part, part, part, part,
        pltpu.VMEM((lmax, 2 * width), F32),
        pltpu.VMEM((lmax, 2 * width), BF),
        pltpu.VMEM((nz, lmax, feat), BF),
        pltpu.VMEM((nz, lmax, feat), BF),
        pltpu.VMEM((2, lmax, feat), F32),
        dma((2, 2, nh, 4)), dma((2, 2, nh, 4)), dma((4,)), dma((4,)), dma((2, nh, 4)), dma((2, nh, 4)), dma((1,)), dma((1,)),
        pltpu.SemaphoreType.REGULAR,
        line, line, line, line,
        dma((1,)), dma((1,)), dma((ny,)), dma((1,)), dma((2, 2)), dma((2, 2)), dma((1,)), dma((ny,)),
        dma((1,)), dma((1,)), dma((ny,)), dma((1,)), dma((2, 2)), dma((2, 2)), dma((1,)), dma((ny,)),
        line, line, line, line,
    ]
    return pl.pallas_call(
        functools.partial(kernel, (nx, nh, ny, nc, nz)),
        out_shape=(
            jax.ShapeDtypeStruct(queries.shape, BF),
            jax.ShapeDtypeStruct(queries.shape, BF),
            jax.ShapeDtypeStruct(encodings.shape, BF),
        ),
        in_specs=[smem, smem] + [vmem] * 5,
        out_specs=(vmem, vmem, vmem),
        scratch_shapes=scratch,
        compiler_params=pltpu.CompilerParams(
            collective_id=0, has_side_effects=True, vmem_limit_bytes=56 * 2**20
        ),
        name="flow_block",
    )(text_length, image_offset, queries, cotangent, encodings, key_weight, value_weight)


def solution(mesh):
    return jax.shard_map(
        functools.partial(shards, mesh.shape["head"]),
        mesh=mesh,
        in_specs=(
            P("seq", "head"),
            P("seq", None, "head"),
            P("seq", "head"),
            P("seq", "head"),
            P("seq"),
            P("seq"),
            P("seq", "head"),
        ),
        out_specs=(P("seq", "head"), P("seq", "head"), P("seq", None, "head")),
        check_vma=False,
    )
```

time: 484 us -> 134 us (0.28)
  waiting for transfers between devices: 392 us -> 0 us
  Pallas kernels: 0 us -> 128 us
  matrix products: 37.7 us -> 0 us
  starting transfers between devices: 27.6 us -> 0 us
  between operations: 15.3 us -> 1.94 us
    all_gather x3 -> x0, waiting for transfers between devices: 307 us -> none  [the longest x1 116 us: shards(): lax.all_gather(value_weight, 'seq', axis=0, tiled=True)]
    pallas_call x0 -> x1, Pallas kernels: none -> 128 us  [shards(): pl.pallas_call(functools.partial(kernel, (nx, nh, ny, nc, nz)), out_shape...]
    reduce_scatter x1 -> x0, waiting for transfers between devices: 74.9 us -> none  [shards(): lax.psum_scatter(partial_grad.astype(jnp.bfloat16), 'head', scatter_dimen...]
    dot_general x9 -> x0, matrix products: 34.6 us -> none  [the longest x1 7.2 us: attend_local(): jnp.einsum('htk,thd->khd', dscores, q, preferred_element_type=jnp.float32)]
    ppermute x4 -> x0, starting transfers between devices: 27.5 us -> none  [passed_along(): lax.ppermute(value, axis, [(source, source + steps) for source in range(l...]
    ppermute x4 -> x0, waiting for transfers between devices: 8.7 us -> none  [passed_along(): lax.ppermute(value, axis, [(source, source + steps) for source in range(l...]
  transfers between devices with their start and end apart: 8 -> 0, of which waited for: 6 -> 0; matrix products, arithmetic and copies ran while one was open for 9% -> 0% of each run, Pallas kernels for 0% -> 0%
where the time goes in v2:
time: 134 us
  Pallas kernels  128 us (96%)
  local copies, waits for them, and re-layouts  3.63 us (3%)
  between operations  1.94 us (1%)
    pallas_call x1, Pallas kernels, shards(): pl.pallas_call(functools.partial(kernel, (nx, nh, ny, nc, nz)), out_shape...  128 us
    unnamed x7, local copies, waits for them, and re-layouts  3.63 us

profile of v2, /device:TPU:24, one launch (start us, length us, event | category | flops | bytes accessed | tf_op | source)
XLA Modules:
  0.0 133.9 jit_solution(4582527393301743862)
XLA Ops:
  1.9 128.4 %flow_block.1 = (bf16[512,384]{1,0:T(8,128)(2,1)}, bf16[512,384]{1,0:T(8,128)(2,1)}, bf16[1,256,512]{2,1,0:T(8,128)(2,1)}) custom-call(s32[1]{0:T(128)S(6)} %copy.13.len_ref, s32[1]{0:T(128)S(6)} %copy.14.off_ref, bf16[512,384]{1,0:T(8,128)(2,1)} %q_ref.1, bf16[512,384]{1,0:T(8,128)(2,1)} %g_ref.1, bf16[1,256,512]{2,1,0:T(8,128)(2,1)} %enc_ref.1, ...), custom_call_target="tpu_custom_call" | custom-call | tf_op jit(solution)/shard_map/flow_block/pallas_call | solution.py:735
  130.3 0.0 copy-start
  130.3 1.8 %copy.15 = bf16[512,384]{1,0:T(8,128)(2,1)} copy(bf16[512,384]{1,0:T(8,128)(2,1)} %get-tuple-element.6) | data formatting | bytes 786432
  132.1 0.0 copy-done
  132.1 0.0 copy-start.1
  132.1 0.7 copy.16
  132.9 0.3 copy-done.1
  133.2 0.7 copy.17
Async XLA Ops:
  130.3 1.8 %copy-start = (bf16[512,384]{1,0:T(8,128)(2,1)S(1)}, bf16[512,384]{1,0:T(8,128)(2,1)}, u32[]{:S(2)}) copy-start(bf16[512,384]{1,0:T(8,128)(2,1)} %get-tuple-element.7) | copy-start | bytes 1179652
  132.1 1.1 copy-start.1

commit v3 on v2

--- a/solution.py
+++ b/solution.py
@@ -11,6 +11,7 @@
 HD = 128
 GRID = (4, 2, 4, 2)
 CHUNKS = 4
+GATE = 7
 BF = jnp.bfloat16
 F32 = jnp.float32
 MESH = pl.DeviceIdType.MESH
@@ -23,8 +24,8 @@
 def kernel(
     dims, len_ref, off_ref, q_ref, g_ref, enc_ref, wk_ref, wv_ref,
     out_ref, dq_ref, de_ref,
-    w, wmid, enc, kv, qg, qp, ro, rn, rp, ra, rm, rc, ba, bm, bc, dkv32, dkv, rr, rl, parts,
-    wss, wrs, wsx, wrx, wsb, wrb, wso, wro, gate,
+    w, mine, wmid, enc, kv, qg, qp, ro, rn, rp, ra, rm, rc, ba, bm, bc, dkv32, dkv, rr, rl, parts,
+    wss, wrs, wts, wtr, wsx, wrx, wsb, wrb, wso, wro, gate,
     esr, err, esl, erl,
     ks, kr, ps, pr, cs, cr, fs, fr,
     bks, bkr, bps, bpr, bcs, bcr, bfs, bfr,
@@ -74,10 +75,9 @@
     near_prev = jnp.logical_and(c == 0, y > 0)
     first_core = c == 0
     second_core = c == nc - 1
-    serves = jnp.logical_or(zh == 1, x < nx - 1)
+    serves = jnp.logical_and(second_core, jnp.logical_or(zh == 1, x < nx - 1))
     served = (at(jnp.where(zh == 1, x, x + 1), zh, 0, 0), h)
-    itself = jnp.logical_and(zh == 1, jnp.logical_and(first_core, y == 0))
-    goes = jnp.logical_not(jnp.logical_and(zh == 1, x == nx - 1))
+    goes = jnp.logical_and(second_core, jnp.logical_not(jnp.logical_and(zh == 1, x == nx - 1)))
     source = (at(x, zh, ny - 1, nc - 1), h)
     source_x = jnp.where(zh == 1, x, x - 1)
 
@@ -95,8 +95,9 @@
         pl.semaphore_signal(barrier, inc=1, device_id=dev, device_id_type=MESH)
 
     hello(sib)
-    hello(up)
-    hello(down)
+    for dev in (up, down):
+        hello(dev)
+        hello((dev[0] + 1 - 2 * c, dev[1]))
 
     @when(h < nz - 1)
     def _():
@@ -114,59 +115,44 @@
     def _():
         hello((s - 1, h))
 
-    @when(first_core)
-    def _():
-        for axis in (0, 1):
-            for way in (1, -1):
-                hello(beside(axis, way)[1])
-
-    @when(serves, jnp.logical_not(itself))
-    def _():
-        hello(served)
-
-    beside_source = jnp.logical_and(goes, jnp.logical_not(far_next))
-
-    @when(beside_source)
-    def _():
-        hello(source)
-
+    for axis in (0, 1):
+        for way in (1, -1):
+            hello(beside(axis, way)[1])
+
+    beside_source = jnp.logical_and(goes, y < ny - 1)
     far_target = jnp.logical_and(far_prev, has_prev)
     far_source = jnp.logical_and(far_next, has_next)
 
+    @when(serves)
+    def _():
+        hello(served)
+
+    @when(beside_source)
+    def _():
+        hello(source)
+
     @when(far_target)
     def _():
         for i in range(ny):
             hello((at(source_x, zh, i, nc - 1), h))
-            if i > 0:
-                hello((at(source_x, zh, i, 0), h))
-
-        @when(zh == 0)
-        def _():
-            hello((at(source_x, zh, 0, 0), h))
 
     @when(far_source)
     def _():
-        for i in range(ny):
-            hello((at(x, zh, i, 0), h))
-            if i < ny - 1:
-                hello((at(x, zh, i, nc - 1), h))
+        for i in range(ny - 1):
+            hello((at(x, zh, i, nc - 1), h))
+
+    mine[:, KC] = wk_ref[...]
+    mine[:, VC] = wv_ref[...]
 
     @when(first_core)
     def _():
         w[x, zh, y, 0, :, KC] = wk_ref[...]
-        w[x, zh, y, 0, :, VC] = wv_ref[...]
 
     @when(second_core)
     def _():
-        wmid[0, :, KC] = wk_ref[...]
-        wmid[0, :, VC] = wv_ref[...]
+        w[x, zh, y, nc - 1, :, VC] = wv_ref[...]
 
     enc[h] = enc_ref[0]
-    own = lax.broadcasted_iota(jnp.int32, (tokens, width), 0) >= off_ref[0]
-    for cols, ref in ((KC, q_ref), (VC, g_ref)):
-        block = ref[...].astype(F32)
-        qg[1, :, cols] = jnp.where(own, block, 0.0).astype(BF)
-        qp[:, cols] = jnp.where(own, 0.0, block).astype(BF)
 
     @when(s == 0)
     def _():
@@ -184,7 +170,7 @@
     def _():
         rl[...] = jnp.zeros_like(rl)
 
-    @when(first_core, jnp.logical_not(serves))
+    @when(second_core, jnp.logical_not(serves))
     def _():
         ba[...] = jnp.zeros_like(ba)
 
@@ -195,32 +181,58 @@
     def n(flag):
         return flag.astype(jnp.int32)
 
-    count = 3 + n(h < nz - 1) + n(h > 0) + n(near_next) + n(near_prev) + 4 * n(first_core)
-    count = count + n(jnp.logical_and(serves, jnp.logical_not(itself))) + n(beside_source)
-    count = count + n(far_target) * (2 * ny - 1 + n(zh == 0)) + n(far_source) * (2 * ny - 1)
+    count = 9 + n(h < nz - 1) + n(h > 0) + n(near_next) + n(near_prev) + n(serves) + n(beside_source)
+    count = count + ny * n(far_target) + (ny - 1) * n(far_source)
     pl.semaphore_wait(barrier, count)
 
-    def lend():
-        return copy(wmid.at[0], w.at[x, zh, y, nc - 1], wso.at[0], wro.at[0], sib)
+    def lend(i):
+        cols = KC if i == 0 else VC
+        return copy(mine.at[:, cols], w.at[x, zh, y, 1 - i, :, cols], wso.at[i], wro.at[i], sib)
 
     def cross(i, leg):
         cols, dev, z_ = (KC, up, zh_down) if i == 0 else (VC, down, zh_up)
-        mid = wmid.at[:, :, cols]
         if leg == 0:
-            return copy(w.at[x, zh, y, :, :, cols], mid, wsx.at[2 * i], wrx.at[2 * i], dev)
-        return copy(mid, w.at[x, z_, y, :, :, cols], wsx.at[2 * i + 1], wrx.at[2 * i + 1], dev)
+            return copy(mine.at[:, cols], wmid.at[:, cols], wsx.at[i, 0], wrx.at[i, 0, 0], dev)
+        return copy(wmid.at[:, cols], w.at[x, z_, y, c, :, cols], wsx.at[i, 1], wrx.at[i, 1, c], (dev[0] - c + i, dev[1]))
+
+    def cross_mid():
+        for i in (0, 1):
+            cross(i, 0).wait_recv()
+            cross(i, 1).start()
+
+    def cross_arrived(i):
+        cols = KC if i == 0 else VC
+        for core in range(nc):
+            ref = w.at[x, 1 - zh, y, core, :, cols]
+            copy(wmid.at[:, cols], ref, wsx.at[i, 1], wrx.at[i, 1, core], sib).wait_recv()
+
+    def block_of(which, stage, z_, index, e, core):
+        cols = KC if which == 0 else VC
+        along_x = which == stage
+        across = e if stage == 0 or isinstance(e, slice) else (place[which][0] + e) % place[which][1]
+        if stage == 0:
+            return w.at[index, z_, y, core, :, cols] if along_x else w.at[x, z_, index, core, :, cols]
+        return w.at[index, z_, across, core, :, cols] if along_x else w.at[across, z_, index, core, :, cols]
+
+    whole = slice(None)
 
     def hop(stage, which, z_, k):
         axis = which if stage == 0 else 1 - which
         index = place[axis][0] if k < 2 else beside(axis, -1 if k == 2 else 1)[0]
         dev = beside(axis, 1 if k % 2 == 0 else -1)[1]
-        cols = KC if which == 0 else VC
-        core = slice(None) if k < 2 else k - 2
-        if axis == 0:
-            ref = w.at[index, z_, y, core, :, cols] if stage == 0 else w.at[index, z_, :, core, :, cols]
-        else:
-            ref = w.at[x, z_, index, core, :, cols] if stage == 0 else w.at[:, z_, index, core, :, cols]
+        ref = block_of(which, stage, z_, index, whole, whole if k < 2 else k - 2)
         return copy(ref, ref, wss.at[stage, which, z_, k], wrs.at[stage, which, z_, k], dev)
+
+    def second(which, z_, k, e):
+        axis = 1 - which
+        ref = block_of(which, 1, z_, place[axis][0], e, whole)
+        dev = beside(axis, 1 if k == 0 else -1)[1]
+        return copy(ref, ref, wts.at[which, z_, k, e], wtr.at[which, z_, k, e], dev)
+
+    def seconds(which, z_, es, act):
+        for e in es:
+            for k in (0, 1):
+                act(second(which, z_, k, e))
 
     def share(which, z_, d):
         here, size = place[1 - which]
@@ -228,75 +240,57 @@
         ref = w.at[:, z_, index, :, :, KC] if which == 0 else w.at[index, z_, :, :, :, VC]
         return copy(ref, ref, wsb.at[which, z_, d], wrb.at[which, z_, d], sib)
 
-    def send(stage, z_, ks_):
-        for which in (0, 1):
-            for k in ks_:
-                hop(stage, which, z_, k).start()
-
-    def receive(stage, z_, ks_):
-        for which in (0, 1):
-            for k in ks_:
-                hop(stage, which, z_, k).wait_recv()
-
-    def shares(z_, ds, act):
-        for which in (0, 1):
-            for d in ds:
-                act(share(which, z_, d))
-
     def start(cp):
         cp.start()
 
+    def arrived(cp):
+        cp.wait_recv()
+
+    def gone(cp):
+        cp.wait_send()
+
+    def firsts(which, z_, ks_, act):
+        for k in ks_:
+            act(hop(0, which, z_, k))
+
+    def lasts(which, z_, act):
+        for k in (2, 3):
+            act(hop(1, which, z_, k))
+
+    def shares(which, z_, ds, act):
+        for d in ds:
+            act(share(which, z_, d))
+
     other = 1 - zh
 
-    def task_a():
-        lend().wait_recv()
-        for i in (0, 1):
-            cross(i, 0).start()
-        send(0, zh, (0, 1))
-
-    def task_b():
-        receive(0, zh, (0, 1))
-        send(0, zh, (2, 3))
-
-    def task_c():
-        for i in (0, 1):
-            cross(i, 0).wait_recv()
-            cross(i, 1).start()
-
-    def task_d():
-        receive(0, zh, (2, 3))
-        send(1, zh, (0, 1))
-
-    def task_e():
-        for i in (0, 1):
-            cross(i, 1).wait_recv()
-        send(0, other, (0, 1))
-
-    def task_f():
-        receive(0, other, (0, 1))
-        send(0, other, (2, 3))
-
-    def task_g():
-        receive(1, zh, (0, 1))
-        send(1, zh, (2, 3))
-        shares(zh, (0, 1, 3), start)
-
-    def task_h():
-        receive(0, other, (2, 3))
-        send(1, other, (0, 1))
-
-    def task_i():
-        receive(1, zh, (2, 3))
-        shares(zh, (2,), start)
-
-    def task_j():
-        receive(1, other, (0, 1))
-        send(1, other, (2, 3))
-        shares(other, (0, 1, 3), start)
-
-    def task_k():
-        receive(1, other, (2, 3))
-        shares(other, (2,), start)
+    def spread(which):
+        def one(z_):
+            firsts(which, z_, (0, 1), start)
+            seconds(which, z_, (0,), start)
+
+        def two(z_):
+            firsts(which, z_, (0, 1), arrived)
+            firsts(which, z_, (2, 3), start)
+            seconds(which, z_, (1, 3), start)
+
+        def three(z_):
+            firsts(which, z_, (2, 3), arrived)
+            seconds(which, z_, (2,), start)
+
+        def four(z_):
+            seconds(which, z_, range(4), arrived)
+            lasts(which, z_, start)
+            shares(which, z_, (0, 1, 3), start)
+
+        def five(z_):
+            lasts(which, z_, arrived)
+            shares(which, z_, (2,), start)
+
+        near = [functools.partial(f, zh) for f in (one, two, three, four, five)]
+        near[0] = lambda: (lend(which).wait_recv(), one(zh))
+        far = [functools.partial(f, other) for f in (one, two, three, four, five)]
+        far[0] = lambda: (cross_arrived(which), one(other))
+        return near, far
 
     def crossing(src, mid, dst, ss, rs, i, leg):
         cols, dev = (KC, up) if i == 0 else (VC, down)
@@ -313,31 +307,29 @@
         return copy(qp, qg.at[0], bks.at[0], bkr.at[0], (s - 1, h))
 
     def back_part(i):
-        return copy(qp.at[pl.ds(i * piece, piece)], ba, bps.at[i], bpr.at[0], (at(source_x, zh, i, 0), h))
+        return copy(qp.at[pl.ds(i * piece, piece)], ba, bps.at[i], bpr.at[0], (at(source_x, zh, i, nc - 1), h))
 
     def back_final(i):
         return copy(bc, qg.at[0, pl.ds(i * piece, piece)], bfs.at[0], bfr.at[i], source)
 
     def back_start():
+        own = lax.broadcasted_iota(jnp.int32, (tokens, width), 0) >= off_ref[0]
+        for cols, ref in ((KC, q_ref), (VC, g_ref)):
+            block = ref[...].astype(F32)
+            qg[1, :, cols] = jnp.where(own, block, 0.0).astype(BF)
+            qp[:, cols] = jnp.where(own, 0.0, block).astype(BF)
+
         @when(has_prev, jnp.logical_not(far_prev))
         def _():
             back_direct().start()
 
         @when(far_target)
         def _():
-            for i in range(1, ny):
+            for i in range(ny):
                 back_part(i).start()
 
-            @when(zh == 0)
-            def _():
-                back_part(0).start()
-
-            @when(zh == 1)
-            def _():
-                ba[...] = qp[:piece, :]
-
     def back_one():
-        @when(serves, jnp.logical_not(itself))
+        @when(serves)
         def _():
             back_part(0).wait_recv()
 
@@ -352,11 +344,15 @@
     def back_three():
         for i in (0, 1):
             back_crossing(i, 1).wait_recv()
-        for i in range(ny):
+        for i in range(ny - 1):
 
             @when(goes, y == i)
             def _():
                 back_final(i).start()
+
+        @when(goes, y == ny - 1)
+        def _():
+            qg[0, (ny - 1) * piece :, :] = bc[...]
 
     def back_arrived():
         @when(has_next)
@@ -367,7 +363,7 @@
 
             @when(far_next)
             def _():
-                for i in range(ny):
+                for i in range(ny - 1):
                     back_final(i).wait_recv()
 
     def send_enc_right(j, r):
@@ -377,6 +373,9 @@
     def send_enc_left(j, r):
         ref = enc.at[j, pl.ds(r * rows, rows)]
         return copy(ref, ref, esl.at[j, r], erl.at[j, r], left)
+
+    def open_gate():
+        pl.semaphore_signal(gate, inc=1, device_id=sib, device_id_type=MESH)
 
     def project(f):
         if nx * nh == nz:
@@ -428,33 +427,59 @@
                         def _():
                             dkv32[...] += project(h + d)
 
-    back_start()
+    for i in (0, 1):
+        cross(i, 0).start()
 
     @when(second_core)
     def _():
-        lend().start()
-        gather({}, False)
-        pl.semaphore_signal(gate, inc=1, device_id=sib, device_id_type=MESH)
-        for z_ in (0, 1):
-            for which in (0, 1):
-                for d in range(4):
-                    share(which, z_, d).wait_recv()
+        lend(0).start()
+        near, far = spread(1)
+        gather(
+            {
+                0: (back_start, near[0]),
+                1: (near[1], cross_mid),
+                2: (near[2],),
+                3: (near[3], back_one),
+                4: (far[0], near[4]),
+                5: (far[1],),
+                6: (far[2], back_two),
+                GATE: (open_gate,),
+            },
+            False,
+        )
+        far[3]()
+        far[4]()
+        back_three()
         dkv32[...] = jnp.zeros_like(dkv32)
-
-        def one(f, carry):
-            dkv32[...] += project(f)
-            return carry
-
-        lax.fori_loop(0, nz, one, 0)
+        if nx * nh == nz:
+            groups = ((zh, nh), (other, nh))
+        else:
+            groups = (None, (0, 1))
+        for z_, group in zip((zh, other), groups):
+            shares(0, z_, range(4), arrived)
+            if group is not None:
+
+                def one(f, carry):
+                    dkv32[...] += project(group[0] + f * group[1])
+                    return carry
+
+                lax.fori_loop(0, nz // group[1], one, 0)
 
     @when(first_core)
     def _():
+        lend(1).start()
+        near, far = spread(0)
         for task in (
-            task_a, task_b, back_one, task_c, task_d, task_e, back_two, task_f, task_g, task_h, task_i, back_three,
+            near[0], back_start, near[1], cross_mid, near[2], near[3], far[0], near[4], far[1], far[2],
         ):
             task()
         pl.semaphore_wait(gate, 1)
-        gather({1: (task_j,), 2: (task_k,)}, True)
+
+        def whole_weights():
+            for z_ in (0, 1):
+                shares(1, z_, range(4), arrived)
+
+        gather({0: (far[3],), 1: (far[4],), 3: (whole_weights,)}, True)
 
     kv[...] = dkv32[...].astype(BF)
 
@@ -580,17 +605,21 @@
                 rl[jl, here, :] = (parts[1, here, :] + rl[jl, here, :].astype(F32)).astype(BF)
                 sum_left(jl, r).start()
 
-        @when(second_core, t == nz // 2)
+        @when(second_core, t == 1)
         def _():
             there_one()
 
+        @when(second_core, t == 3)
+        def _():
+            there_two()
+
+        @when(second_core, t == 5)
+        def _():
+            there_three()
+
         return carry
 
     lax.fori_loop(0, nz - 1, reduce_step, 0)
-
-    @when(second_core)
-    def _():
-        there_two()
 
     parts[0] = partial(h)
     for r in range(CHUNKS):
@@ -607,10 +636,6 @@
         total = parts[0, here, :] + rr[h, here, :].astype(F32) + rl[h, here, :].astype(F32)
         de_ref[0, here, :] = total.astype(BF)
 
-    @when(second_core)
-    def _():
-        there_three()
-
     @when(has_prev)
     def _():
         @when(jnp.logical_not(far_prev))
@@ -626,30 +651,34 @@
     for cols, ref in ((KC, out_ref), (VC, dq_ref)):
         ref[...] = jnp.where(own, ro[:, cols].astype(F32), rp[:, cols].astype(F32)).astype(BF)
 
+    for i in (0, 1):
+        for leg in (0, 1):
+            cross(i, leg).wait_send()
+
+    def weights_gone(which):
+        lend(1 - which).wait_send()
+        for z_ in (0, 1):
+            shares(which, z_, range(4), gone)
+            firsts(which, z_, range(4), gone)
+            seconds(which, z_, range(4), gone)
+            lasts(which, z_, gone)
+
     @when(first_core)
     def _():
-        for z_ in (0, 1):
-            for which in (0, 1):
-                for d in range(4):
-                    share(which, z_, d).wait_send()
-                    for stage in (0, 1):
-                        hop(stage, which, z_, d).wait_send()
+        weights_gone(0)
+
+    @when(second_core)
+    def _():
+        weights_gone(1)
         for i in (0, 1):
             for leg in (0, 1):
-                cross(i, leg).wait_send()
                 back_crossing(i, leg).wait_send()
-
-        @when(goes)
+                there_crossing(i, leg).wait_send()
+
+        @when(goes, y < ny - 1)
         def _():
             back_final(0).wait_send()
 
-    @when(second_core)
-    def _():
-        lend().wait_send()
-        for i in (0, 1):
-            for leg in (0, 1):
-                there_crossing(i, leg).wait_send()
-
         @when(serves)
         def _():
             there_final(0).wait_send()
@@ -660,12 +689,8 @@
 
     @when(far_target)
     def _():
-        for i in range(1, ny):
+        for i in range(ny):
             back_part(i).wait_send()
-
-        @when(zh == 0)
-        def _():
-            back_part(0).wait_send()
 
     @when(has_next, jnp.logical_not(far_next))
     def _():
@@ -714,7 +739,8 @@
     line = dma((nz, CHUNKS))
     scratch = [
         pltpu.VMEM((nx, nh, ny, nc, depth, 2 * width), BF),
-        pltpu.VMEM((nc, depth, 2 * width), BF),
+        pltpu.VMEM((depth, 2 * width), BF),
+        pltpu.VMEM((depth, 2 * width), BF),
         pltpu.VMEM((nz, lmax, feat), BF),
         pltpu.VMEM((lmax, 2 * width), BF),
         pltpu.VMEM((2, tokens, 2 * width), BF),
@@ -725,7 +751,8 @@
         pltpu.VMEM((nz, lmax, feat), BF),
         pltpu.VMEM((nz, lmax, feat), BF),
         pltpu.VMEM((2, lmax, feat), F32),
-        dma((2, 2, nh, 4)), dma((2, 2, nh, 4)), dma((4,)), dma((4,)), dma((2, nh, 4)), dma((2, nh, 4)), dma((1,)), dma((1,)),
+        dma((2, 2, nh, 4)), dma((2, 2, nh, 4)), dma((2, nh, 2, 4)), dma((2, nh, 2, 4)), dma((2, 2)), dma((2, 2, nc)),
+        dma((2, nh, 4)), dma((2, nh, 4)), dma((2,)), dma((2,)),
         pltpu.SemaphoreType.REGULAR,
         line, line, line, line,
         dma((1,)), dma((1,)), dma((ny,)), dma((1,)), dma((2, 2)), dma((2, 2)), dma((1,)), dma((ny,)),
@@ -735,9 +762,9 @@
     return pl.pallas_call(
         functools.partial(kernel, (nx, nh, ny, nc, nz)),
         out_shape=(
-            jax.ShapeDtypeStruct(queries.shape, BF),
-            jax.ShapeDtypeStruct(queries.shape, BF),
-            jax.ShapeDtypeStruct(encodings.shape, BF),
+            pltpu.VMEM(queries.shape, BF),
+            pltpu.VMEM(queries.shape, BF),
+            pltpu.VMEM(encodings.shape, BF),
         ),
         in_specs=[smem, smem] + [vmem] * 5,
         out_specs=(vmem, vmem, vmem),

time: 134 us -> 128 us (0.955); the launches traced: 134 us -> 126 us
  Pallas kernels: 128 us -> 122 us
  local copies, waits for them, and re-layouts: 3.63 us -> 2.2 us
    pallas_call x1, Pallas kernels: 128 us -> 122 us  [shards(): pl.pallas_call(functools.partial(kernel, (nx, nh, ny, nc, nz)), out_shape...]
    unnamed x7 -> x3, local copies, waits for them, and re-layouts: 3.63 us -> 2.2 us
where the time goes in v3:
time: 128 us; the launch traced here: 126 us
  Pallas kernels  122 us (95%)
  local copies, waits for them, and re-layouts  2.2 us (2%)
  between operations  1.93 us (2%)
    pallas_call x1, Pallas kernels, shards(): pl.pallas_call(functools.partial(kernel, (nx, nh, ny, nc, nz)), out_shape...  122 us

profile of v3, /device:TPU:24, one launch (start us, length us, event | category | flops | bytes accessed | tf_op | source)
XLA Modules:
  0.0 125.9 jit_solution(617913355347605081)
XLA Ops:
  1.9 121.8 %flow_block.1 = (bf16[512,384]{1,0:T(8,128)(2,1)S(1)}, bf16[512,384]{1,0:T(8,128)(2,1)S(1)}, bf16[1,256,512]{2,1,0:T(8,128)(2,1)S(1)}) custom-call(s32[1]{0:T(128)S(6)} %copy.16.len_ref, s32[1]{0:T(128)S(6)} %copy.17.off_ref, bf16[512,384]{1,0:T(8,128)(2,1)} %q_ref.1, bf16[512,384]{1,0:T(8,128)(2,1)} %g_ref.1, bf16[1,256,512]{2,1,0:T(8,128)(2,1)} %enc_ref.1, ...), custom_call_target="tpu_custom_call" | custom-call | tf_op jit(solution)/shard_map/flow_block/pallas_call | solution.py:762
  123.7 0.7 copy.13
  124.5 0.7 copy.15
  125.2 0.7 copy.14

commit v4 on v3

--- a/solution.py
+++ b/solution.py
@@ -11,7 +11,7 @@
 HD = 128
 GRID = (4, 2, 4, 2)
 CHUNKS = 4
-GATE = 7
+GATE = 6
 BF = jnp.bfloat16
 F32 = jnp.float32
 MESH = pl.DeviceIdType.MESH
@@ -442,8 +442,7 @@
                 3: (near[3], back_one),
                 4: (far[0], near[4]),
                 5: (far[1],),
-                6: (far[2], back_two),
-                GATE: (open_gate,),
+                GATE: (far[2], back_two, open_gate),
             },
             False,
         )
@@ -459,11 +458,12 @@
             shares(0, z_, range(4), arrived)
             if group is not None:
 
-                def one(f, carry):
-                    dkv32[...] += project(group[0] + f * group[1])
+                def two(f, carry):
+                    first, step = group
+                    dkv32[...] += project(first + 2 * f * step) + project(first + (2 * f + 1) * step)
                     return carry
 
-                lax.fori_loop(0, nz // group[1], one, 0)
+                lax.fori_loop(0, nz // (2 * group[1]), two, 0)
 
     @when(first_core)
     def _():
@@ -496,12 +496,13 @@
             g = qg[b, :, vc]
             k = kv[:, kc]
             v = kv[:, vc]
-            scores = jnp.where(ok, dot(q, k, 1, 1) * scale, -1e30)
-            expo = jnp.exp(scores - jnp.max(scores, axis=-1, keepdims=True))
-            probs = expo / jnp.sum(expo, axis=-1, keepdims=True)
+            scores = jnp.where(ok, dot(q, k, 1, 1), -1e30)
+            expo = jnp.exp2((scores - jnp.max(scores, axis=-1, keepdims=True)) * (scale * math.log2(math.e)))
+            inverse = 1.0 / jnp.sum(expo, axis=-1, keepdims=True)
+            probs = expo * inverse
             dprobs = dot(g, v, 1, 1)
             delta = jnp.sum(probs * dprobs, axis=-1, keepdims=True)
-            ds = (probs * (dprobs - delta) * scale).astype(BF)
+            ds = ((expo * (inverse * scale)) * (dprobs - delta)).astype(BF)
             pb = probs.astype(BF)
             result[:, kc] = dot(pb, v, 1, 0).astype(BF)
             result[:, vc] = dot(ds, k, 1, 0).astype(BF)

time: 128 us -> 126 us (0.984)
  no operation moved by 1% of the time
where the time goes in v4:
time: 126 us; the launch traced here: 125 us
  Pallas kernels  121 us (96%)
  local copies, waits for them, and re-layouts  2.2 us (2%)
  between operations  1.93 us (2%)
    pallas_call x1, Pallas kernels, shards(): pl.pallas_call(functools.partial(kernel, (nx, nh, ny, nc, nz)), out_shape...  121 us

profile of v4, /device:TPU:24, one launch (start us, length us, event | category | flops | bytes accessed | tf_op | source)
XLA Modules:
  0.0 124.9 jit_solution(5320989948385525450)
XLA Ops:
  1.9 120.7 %flow_block.1 = (bf16[512,384]{1,0:T(8,128)(2,1)S(1)}, bf16[512,384]{1,0:T(8,128)(2,1)S(1)}, bf16[1,256,512]{2,1,0:T(8,128)(2,1)S(1)}) custom-call(s32[1]{0:T(128)S(6)} %copy.16.len_ref, s32[1]{0:T(128)S(6)} %copy.17.off_ref, bf16[512,384]{1,0:T(8,128)(2,1)} %q_ref.1, bf16[512,384]{1,0:T(8,128)(2,1)} %g_ref.1, bf16[1,256,512]{2,1,0:T(8,128)(2,1)} %enc_ref.1, ...), custom_call_target="tpu_custom_call" | custom-call | tf_op jit(solution)/shard_map/flow_block/pallas_call | solution.py:763
  122.7 0.7 copy.13
  123.4 0.7 copy.15
  124.1 0.7 copy.14

commit v5 on v4

--- a/solution.py
+++ b/solution.py
@@ -418,12 +418,17 @@
                     if d == 0:
                         dkv32[...] = project(h)
                     else:
-
-                        @when(h - d >= 0)
+                        low, high = h - d >= 0, h + d < nz
+
+                        @when(low, high)
+                        def _():
+                            dkv32[...] += project(h - d) + project(h + d)
+
+                        @when(low, jnp.logical_not(high))
                         def _():
                             dkv32[...] += project(h - d)
 
-                        @when(h + d < nz)
+                        @when(high, jnp.logical_not(low))
                         def _():
                             dkv32[...] += project(h + d)
 

time: 126 us -> 126 us (level)
  no operation moved by 1% of the time
where the time goes in v5:
time: 126 us; the launch traced here: 125 us
  Pallas kernels  121 us (96%)
  local copies, waits for them, and re-layouts  2.2 us (2%)
  between operations  1.93 us (2%)
    pallas_call x1, Pallas kernels, shards(): pl.pallas_call(functools.partial(kernel, (nx, nh, ny, nc, nz)), out_shape...  121 us

profile of v5, /device:TPU:24, one launch (start us, length us, event | category | flops | bytes accessed | tf_op | source)
XLA Modules:
  0.0 124.9 jit_solution(8059746704456799749)
XLA Ops:
  1.9 120.7 %flow_block.1 = (bf16[512,384]{1,0:T(8,128)(2,1)S(1)}, bf16[512,384]{1,0:T(8,128)(2,1)S(1)}, bf16[1,256,512]{2,1,0:T(8,128)(2,1)S(1)}) custom-call(s32[1]{0:T(128)S(6)} %copy.16.len_ref, s32[1]{0:T(128)S(6)} %copy.17.off_ref, bf16[512,384]{1,0:T(8,128)(2,1)} %q_ref.1, bf16[512,384]{1,0:T(8,128)(2,1)} %g_ref.1, bf16[1,256,512]{2,1,0:T(8,128)(2,1)} %enc_ref.1, ...), custom_call_target="tpu_custom_call" | custom-call | tf_op jit(solution)/shard_map/flow_block/pallas_call | solution.py:768
  122.7 0.7 copy.13
  123.4 0.7 copy.15
  124.1 0.7 copy.14
